TPU v7x, 256 devices: a whole 4x4x8 slice. The times are simulated.
256 devices in a mesh: gx: 8 (over y_lo, x), gy: 32 (over z, y_hi, core).
Axes of the slice: x: 4, y: 4 (y_hi: 2, y_lo: 2; y = y_hi * 2 + y_lo), z: 8, core: 2. Of those that a mesh axis runs over, the one named last changes fastest.
Arguments:
- segments: float32 [9, 2097152], P(None, ('gx', 'gy')), as said below
- pair_list: int32 [131072, 2], P(('gx', 'gy')), may hold values from 0 to 127, as said below
- pair_count: int32 [256], P(('gx', 'gy')), may hold values from 64 to 512
- send_list: int32 [1024, 16], P(('gx', 'gy')), may hold values from 0 to 63, as said below
- cell_ids: int32 [2097152], P(('gx', 'gy')), may hold values from 0 to 511, as said below
Outputs:
- forces: float32 [3, 2097152], P(None, ('gx', 'gy'))
Inputs may be any that keep to these rules, and one draw needn't show every extreme that they name: `pair_list`: column 0 names a block below 64. Column 1 names another block of the same device (below 64, never equal to column 0), or a received block 64 + k*16 + j only where the neighbour of side k exists. `send_list`: each row names 16 different blocks of the sending device. `cell_ids`: segments of device d lie in cells d*2 to d*2 + 1. `segments`: the midpoints of device d (gx index ix, gy index iy) lie in [ix, ix + 1) x [iy, iy + 1) x [0, 1).
All inputs are finite; a program needn't handle non-finite values.
Results may differ from a plain program's by a relative error of at most 0.0001.
Values sent between devices are 32-bit elements; how exact they have to be, the bound alone decides.
A program may use at most 64 MiB of HBM per device.

v0:
```python
import math

import jax
import jax.numpy as jnp
from jax import lax
from jax.sharding import PartitionSpec as P

BLOCK = 128
CELL_DEV = 2


strength = 0.2
core_sq = 0.05
far_gain = 0.5
far_core_sq = 0.1


def extended(block, sides, width):
    for axis, dim in sides:
        count = lax.axis_size(axis)
        forward = [(i, i + 1) for i in range(count - 1)]
        backward = [(target, source) for source, target in forward]
        low = lax.ppermute(
            lax.slice_in_dim(block, block.shape[dim] - width, None, axis=dim), axis, forward
        )
        high = lax.ppermute(lax.slice_in_dim(block, 0, width, axis=dim), axis, backward)
        block = jnp.concatenate([low, block, high], axis=dim)
    return block


def pair_terms(first, second, live_mask):
    offset = first[:, 0:3, :, None] - second[:, 0:3, None, :]
    dist_sq = jnp.sum(offset * offset, axis=1) + core_sq
    burgers_dot = jnp.sum(first[:, 6:9, :, None] * second[:, 6:9, None, :], axis=1)
    line_dot = jnp.sum(first[:, 3:6, :, None] * second[:, 3:6, None, :], axis=1)
    coupling = (
        strength * burgers_dot * line_dot / (dist_sq * jnp.sqrt(dist_sq)) * live_mask[:, None, None]
    )
    pushed = coupling[:, None] * offset
    return (jnp.sum(pushed, axis=3), -jnp.sum(pushed, axis=2))


def cell_centers(cell_total, per_device, span_y):
    cell_index = jnp.arange(cell_total, dtype=jnp.int32)
    device = cell_index // per_device
    sub_cell = (cell_index % per_device).astype(jnp.float32)
    centre_x = (device // span_y).astype(jnp.float32) + 0.5
    centre_y = (device % span_y).astype(jnp.float32) + (sub_cell + 0.5) / per_device
    centre_z = jnp.full((cell_total,), 0.5, jnp.float32)
    return jnp.stack([centre_x, centre_y, centre_z])


def far_terms(position, weight, moments, centers):
    offset = position[:, :, None] - centers[:, None, :]
    dist_sq = jnp.sum(offset * offset, axis=0) + far_core_sq
    falloff = moments[None, :] / (dist_sq * jnp.sqrt(dist_sq))
    return far_gain * weight[None, :] * jnp.sum(falloff[None] * offset, axis=2)


def body(segments, pair_list, pair_count, send_list, cell_ids):
    block_count = segments.shape[1] // BLOCK
    ghost_count = send_list.shape[1]
    own_blocks = segments.reshape(9, block_count, BLOCK).transpose(1, 0, 2)
    leaving_x = jnp.take(own_blocks, send_list[0:2].reshape(-1), axis=0)
    arrived_x = extended(leaving_x, (("gx", 0),), ghost_count)
    leaving_y = jnp.take(own_blocks, send_list[2:4].reshape(-1), axis=0)
    arrived_y = extended(leaving_y, (("gy", 0),), ghost_count)
    ghosts = jnp.concatenate(
        [
            arrived_x[:ghost_count],
            arrived_x[3 * ghost_count :],
            arrived_y[:ghost_count],
            arrived_y[3 * ghost_count :],
        ],
        axis=0,
    )
    all_blocks = jnp.concatenate([own_blocks, ghosts], axis=0)
    forces = jnp.zeros((block_count + 4 * ghost_count, 3, BLOCK), jnp.float32)
    batch_size = min(16, pair_list.shape[0])
    live_pairs = pair_count[0]
    turn_count = (live_pairs + batch_size - 1) // batch_size

    def add_pairs(turn, forces):
        pair_rows = lax.dynamic_slice_in_dim(pair_list, turn * batch_size, batch_size, 0)
        first_ids = pair_rows[:, 0]
        second_ids = pair_rows[:, 1]
        live_mask = (
            turn * batch_size + jnp.arange(batch_size, dtype=jnp.int32) < live_pairs
        ).astype(jnp.float32)
        force_first, force_second = pair_terms(
            all_blocks[first_ids], all_blocks[second_ids], live_mask
        )
        return forces.at[first_ids].add(force_first).at[second_ids].add(force_second)

    forces = lax.fori_loop(0, turn_count, add_pairs, forces)
    self_size = min(16, block_count)

    def add_self(turn, forces):
        start = turn * self_size
        group = lax.dynamic_slice_in_dim(all_blocks, start, self_size, 0)
        force_first, _ = pair_terms(group, group, jnp.ones((self_size,), jnp.float32))
        current = lax.dynamic_slice_in_dim(forces, start, self_size, 0)
        return lax.dynamic_update_slice_in_dim(forces, current + force_first, start, 0)

    forces = lax.fori_loop(0, block_count // self_size, add_self, forces)
    back_x = extended(
        forces[block_count : block_count + 2 * ghost_count], (("gx", 0),), ghost_count
    )
    back_y = extended(forces[block_count + 2 * ghost_count :], (("gy", 0),), ghost_count)
    own_forces = forces[:block_count]
    own_forces = (
        own_forces.at[send_list[0]]
        .add(back_x[:ghost_count])
        .at[send_list[1]]
        .add(back_x[3 * ghost_count :])
    )
    own_forces = (
        own_forces.at[send_list[2]]
        .add(back_y[:ghost_count])
        .at[send_list[3]]
        .add(back_y[3 * ghost_count :])
    )
    pair_force = own_forces.transpose(1, 0, 2).reshape(3, -1)
    weight = jnp.sum(segments[3:6] * segments[6:9], axis=0)
    span_x = lax.axis_size("gx")
    span_y = lax.axis_size("gy")
    cell_total = CELL_DEV * span_x * span_y
    moments = lax.psum(jax.ops.segment_sum(weight, cell_ids, cell_total), ("gx", "gy"))
    centers = cell_centers(cell_total, CELL_DEV, span_y)
    seg_count = segments.shape[1]
    far_size = math.gcd(seg_count, 1024)
    positions = segments[0:3].reshape(3, -1, far_size).transpose(1, 0, 2)
    weights = weight.reshape(-1, far_size)
    far_force = lax.map(
        lambda items: far_terms(items[0], items[1], moments, centers), (positions, weights)
    )
    far_force = far_force.transpose(1, 0, 2).reshape(3, seg_count)
    return pair_force + far_force


def solution(mesh):
    in_specs = (
        P(None, ("gx", "gy")),
        P(("gx", "gy"), None),
        P(("gx", "gy")),
        P(("gx", "gy"), None),
        P(("gx", "gy")),
    )
    out_specs = P(None, ("gx", "gy"))
    return jax.shard_map(body, mesh=mesh, in_specs=in_specs, out_specs=out_specs, check_vma=False)
```

profile of v0, /device:TPU:75, one launch (start us, length us, event | category | flops | bytes accessed | tf_op | source)
XLA Modules:
  0.0 548.3 jit_solution(4225696967027645283)
XLA Ops:
  0.9 1.1 copy.18
  3.1 3.1 collective-permute-start
  6.2 2.2 collective-permute-start.1
  9.1 5.0 collective-permute-start.2
  14.2 1.9 collective-permute-start.3
  16.3 57.2 %scatter_custom_fusion.6 = f32[512]{0:T(512)S(1)} fusion(s32[8192]{0:T(1024)} %param.17, f32[8192]{0:T(1024)S(1)} %get-tuple-element.195, f32[]{:T(128)} %constant.160.clone.1), kind=kCustom, calls=%fused_computation.88 | custom fusion | flops 8192 | bytes 2560 | tf_op jit(solution)/shard_map/scatter-add | solution.py:128
  73.5 76.0 %psum.7 = f32[512]{0:T(512)S(1)} all-reduce(f32[512]{0:T(512)S(1)} %scatter_custom_fusion.6), channel_id=1, replica_groups=mesh['gx'=8,'gy'=32] {'gx','gy'}, use_global_device_ids=true, to_apply=%region_21.23 | all-reduce | flops 512 | bytes 4096 | tf_op jit(solution)/shard_map/psum | solution.py:128
  149.5 24.2 %while.35 = (s32[]{:T(128)}, f32[8,3,1024]{2,1,0:T(4,128)S(1)}, f32[8,1024]{1,0:T(8,128)S(1)}, f32[512]{0:T(512)S(1)}, f32[8,3,1024]{2,1,0:T(4,128)S(1)}, /*index=5*/f32[3,512]{1,0:T(4,128)S(1)}, s32[]{:T(128)}) while((s32[]{:T(128)}, f32[8,3,1024]{2,1,0:T(4,128)S(1)}, f32[8,1024]{1,0:T(8,128)S(1)}, f32[512]{0:T(512)S(1)}, ...), condition=%wide.region_25.27_spmd, body=%wide.region_22.26_spmd.sunk | while | flops 10486786 | bytes 8509529 | solution.py:134
  151.2 1.2 fusion.57
  154.2 1.2 fusion.57
  157.3 1.2 fusion.57
  160.3 1.2 fusion.57
  163.3 1.2 fusion.57
  166.4 1.2 fusion.57
  169.4 1.2 fusion.57
  172.4 1.2 fusion.57
  174.7 137.6 %while.33 = (s32[]{:T(128)}, f32[128,3,128]{2,1,0:T(4,128)S(1)}, s32[]{:T(128)}, s32[512,2]{0,1:T(2,128)}, f32[128,9,128]{2,1,0:T(8,128)S(1)}, /*index=5*/s32[]{:T(128)}, s32[]{:T(128)}, s32[]{:T(128)}, s32[]{:T(128)}, s32[]{:T(128)}) while((s32[]{:T(128)}, f32[128,3,128]{2,1,0:T(4,128)S(1)}, s32[]{:T(128)}, s32[512,2]{0,1:T(2,128)}, ...), condition=%wide.region_8.10_spmd, body=%wide.region_0.9_spmd.sunk | while | flops 9445526 | bytes 9430175 | solution.py:95
  181.0 2.0 fusion.51
  183.1 1.1 scatter_fusion
  191.6 2.0 fusion.51
  193.6 1.1 scatter_fusion
  202.1 2.0 fusion.51
  204.2 1.1 scatter_fusion
  205.3 1.1 scatter_fusion.1
  212.7 2.0 fusion.51
  214.8 1.1 scatter_fusion
  215.9 1.1 scatter_fusion.1
  223.3 2.0 fusion.51
  225.4 1.1 scatter_fusion
  226.5 1.1 scatter_fusion.1
  233.9 2.0 fusion.51
  235.9 1.1 scatter_fusion
  237.0 1.1 scatter_fusion.1
  244.4 2.0 fusion.51
  246.5 1.1 scatter_fusion
  247.6 1.1 scatter_fusion.1
  255.0 2.0 fusion.51
  257.1 1.1 scatter_fusion
  265.6 2.0 fusion.51
  267.6 1.1 scatter_fusion
  276.1 2.0 fusion.51
  278.2 1.1 scatter_fusion
  286.7 2.0 fusion.51
  288.8 1.1 scatter_fusion
  297.3 2.0 fusion.51
  299.3 1.1 scatter_fusion
  300.4 1.1 scatter_fusion.1
  307.8 2.0 fusion.51
  309.9 1.1 scatter_fusion
  312.3 22.1 %while.34 = (s32[]{:T(128)}, f32[128,3,128]{2,1,0:T(4,128)S(1)}, f32[128,9,128]{2,1,0:T(8,128)S(1)}, s32[]{:T(128)}, s32[]{:T(128)}, /*index=5*/s32[]{:T(128)}, s32[]{:T(128)}, s32[]{}, s32[]{}) while((s32[]{:T(128)}, f32[128,3,128]{2,1,0:T(4,128)S(1)}, f32[128,9,128]{2,1,0:T(8,128)S(1)}, s32[]{:T(128)}, s32[]{:T(128)}, ...), condition=%wide.region_14.16_spmd, body=%wide.region_9.15_spmd.sunk | while | flops 8388616 | bytes 8757427 | solution.py:105
  312.4 2.1 fusion.52
  316.0 1.9 fusion.54
  317.9 2.1 fusion.52
  321.5 1.9 fusion.54
  323.4 2.1 fusion.52
  327.0 1.9 fusion.54
  329.0 2.1 fusion.52
  332.5 1.9 fusion.54
  334.5 1.9 collective-permute-start.4
  336.4 3.4 collective-permute-start.5
  339.8 37.3 %collective-permute-start.6 = (f32[16,3,128]{2,1,0:T(4,128)S(1)}, f32[16,3,128]{2,1,0:T(4,128)S(1)}, u32[]{:S(2)}, u32[]{:S(2)}) collective-permute-start(f32[16,3,128]{2,1,0:T(4,128)S(1)} %get-tuple-element.197), channel_id=1, source_target_pairs={{0,1},{1,2},{2,3},{3,4},{4,5},{5,6},{6,7},{7,8},{8,9},{9,10},{10,1... | collective-permute-start | bytes 73736 | tf_op jit(solution)/shard_map/ppermute | solution.py:23
  377.1 1.9 collective-permute-start.7
  379.1 1.1 scatter_fusion.2
  382.4 164.1 %collective-permute-done.7 = f32[16,3,128]{2,1,0:T(4,128)S(1)} collective-permute-done((f32[16,3,128]{2,1,0:T(4,128)S(1)}, f32[16,3,128]{2,1,0:T(4,128)S(1)}, u32[]{:S(2)}, u32[]{:S(2)}) %collective-permute-start.7) | collective-permute-done | bytes 24608 | tf_op jit(solution)/shard_map/ppermute | solution.py:26
  (278 shorter events, 115.6 us)
Async XLA Ops:
  2.1 14.0 %copy-start = (f32[9,8192]{1,0:T(8,128)S(1)}, f32[9,8192]{1,0:T(8,128)}, u32[]{:S(2)}) copy-start(f32[9,8192]{1,0:T(8,128)} %param.13) | copy-start | bytes 884740
  3.1 171.5 %collective-permute-start = (f32[16,9,128]{2,1,0:T(8,128)S(1)}, f32[16,9,128]{2,1,0:T(8,128)S(1)}, u32[]{:S(2)}, u32[]{:S(2)}) collective-permute-start(f32[16,9,128]{2,1,0:T(8,128)S(1)} %get-tuple-element.203), channel_id=1, source_target_pairs={{0,32},{32,64},{64,96},{96,128},{128,160},{160,192},{192,224},{1,3... | collective-permute-start | bytes 221192 | tf_op jit(solution)/shard_map/ppermute | solution.py:23
  6.2 168.4 %collective-permute-start.1 = (f32[16,9,128]{2,1,0:T(8,128)S(1)}, f32[16,9,128]{2,1,0:T(8,128)S(1)}, u32[]{:S(2)}, u32[]{:S(2)}) collective-permute-start(f32[16,9,128]{2,1,0:T(8,128)S(1)} %get-tuple-element.202), channel_id=1, source_target_pairs={{32,0},{64,32},{96,64},{128,96},{160,128},{192,160},{224,192},{33,... | collective-permute-start | bytes 221192 | tf_op jit(solution)/shard_map/ppermute | solution.py:26
  9.1 165.5 %collective-permute-start.2 = (f32[16,9,128]{2,1,0:T(8,128)S(1)}, f32[16,9,128]{2,1,0:T(8,128)S(1)}, u32[]{:S(2)}, u32[]{:S(2)}) collective-permute-start(f32[16,9,128]{2,1,0:T(8,128)S(1)} %get-tuple-element.201), channel_id=1, source_target_pairs={{0,1},{1,2},{2,3},{3,4},{4,5},{5,6},{6,7},{7,8},{8,9},{9,10},{10,1... | collective-permute-start | bytes 221192 | tf_op jit(solution)/shard_map/ppermute | solution.py:23
  14.2 160.5 %collective-permute-start.3 = (f32[16,9,128]{2,1,0:T(8,128)S(1)}, f32[16,9,128]{2,1,0:T(8,128)S(1)}, u32[]{:S(2)}, u32[]{:S(2)}) collective-permute-start(f32[16,9,128]{2,1,0:T(8,128)S(1)} %get-tuple-element.200), channel_id=1, source_target_pairs={{1,0},{2,1},{3,2},{4,3},{5,4},{6,5},{7,6},{8,7},{9,8},{10,9},{11,1... | collective-permute-start | bytes 221192 | tf_op jit(solution)/shard_map/ppermute | solution.py:26
  312.3 66.7 %copy-start.1 = (s32[4,16]{1,0:T(4,128)S(1)}, s32[4,16]{1,0:T(4,128)}, u32[]{:S(2)}) copy-start(s32[4,16]{1,0:T(4,128)} %param.16) | copy-start | bytes 772
  334.5 44.6 %collective-permute-start.4 = (f32[16,3,128]{2,1,0:T(4,128)S(1)}, f32[16,3,128]{2,1,0:T(4,128)S(1)}, u32[]{:S(2)}, u32[]{:S(2)}) collective-permute-start(f32[16,3,128]{2,1,0:T(4,128)S(1)} %get-tuple-element.199), channel_id=1, source_target_pairs={{0,32},{32,64},{64,96},{96,128},{128,160},{160,192},{192,224},{1,3... | collective-permute-start | bytes 73736 | tf_op jit(solution)/shard_map/ppermute | solution.py:23
  336.4 43.8 %collective-permute-start.5 = (f32[16,3,128]{2,1,0:T(4,128)S(1)}, f32[16,3,128]{2,1,0:T(4,128)S(1)}, u32[]{:S(2)}, u32[]{:S(2)}) collective-permute-start(f32[16,3,128]{2,1,0:T(4,128)S(1)} %get-tuple-element.198), channel_id=1, source_target_pairs={{32,0},{64,32},{96,64},{128,96},{160,128},{192,160},{224,192},{33,... | collective-permute-start | bytes 73736 | tf_op jit(solution)/shard_map/ppermute | solution.py:26
  339.8 41.6 %collective-permute-start.6 = (f32[16,3,128]{2,1,0:T(4,128)S(1)}, f32[16,3,128]{2,1,0:T(4,128)S(1)}, u32[]{:S(2)}, u32[]{:S(2)}) collective-permute-start(f32[16,3,128]{2,1,0:T(4,128)S(1)} %get-tuple-element.197), channel_id=1, source_target_pairs={{0,1},{1,2},{2,3},{3,4},{4,5},{5,6},{6,7},{7,8},{8,9},{9,10},{10,1... | collective-permute-start | bytes 73736 | tf_op jit(solution)/shard_map/ppermute | solution.py:23
  377.1 169.4 %collective-permute-start.7 = (f32[16,3,128]{2,1,0:T(4,128)S(1)}, f32[16,3,128]{2,1,0:T(4,128)S(1)}, u32[]{:S(2)}, u32[]{:S(2)}) collective-permute-start(f32[16,3,128]{2,1,0:T(4,128)S(1)} %get-tuple-element.196), channel_id=1, source_target_pairs={{1,0},{2,1},{3,2},{4,3},{5,4},{6,5},{7,6},{8,7},{9,8},{10,9},{11,1... | collective-permute-start | bytes 73736 | tf_op jit(solution)/shard_map/ppermute | solution.py:26
where the time goes:
time: 552 us; the launch traced here: 548 us
  other arithmetic  219 us (40%)
  waiting for transfers between devices  164 us (30%)
  blocking collectives  76 us (14%)
  starting transfers between devices  56.8 us (10%)
  local copies, waits for them, and re-layouts  29 us (5%)
    ppermute x4, waiting for transfers between devices, extended(): lax.ppermute(lax.slice_in_dim(block, 0, width, axis=dim), axis, backward)  164 us
    psum x1, blocking collectives, body(): lax.psum(jax.ops.segment_sum(weight, cell_ids, cell_total), ('gx', 'gy'))  76 us
    scatter-add x1, other arithmetic, body(): jax.ops.segment_sum(weight, cell_ids, cell_total)  57.2 us
    ppermute x4, starting transfers between devices, extended(): lax.ppermute(lax.slice_in_dim(block, block.shape[dim] - width, None, axis...  47.4 us
    reduce_sum x17, other arithmetic, pair_terms(): return (jnp.sum(pushed, axis=3), -jnp.sum(pushed, axis=2))  34 us
    scatter-add x26, other arithmetic, add_pairs(): forces.at[first_ids].add(force_first).at[second_ids].add(force_second)  28.4 us
    reduce_sum x17, other arithmetic, pair_terms(): dist_sq = jnp.sum(offset * offset, axis=1) + core_sq  21.8 us
    reduce_sum x17, other arithmetic, pair_terms(): jnp.sum(first[:, 6:9, :, None] * second[:, 6:9, None, :], axis=1)  17.6 us
  transfers between devices with their start and end apart: 8, of which 1 were waited for; matrix products, arithmetic and copies ran while one was open for 16% of the time, Pallas kernels for 0%

commit v1 on v0

v1 whole, which is shorter than its diff:
```python
import functools

import jax
import jax.numpy as jnp
from jax import lax
from jax.experimental import pallas as pl
from jax.experimental.pallas import tpu as pltpu
from jax.sharding import PartitionSpec as P

f32, bf16, i32 = jnp.float32, jnp.bfloat16, jnp.int32
MESH = pl.DeviceIdType.MESH
BLOCK = 128
OWN = 64
GHOST = 16
ALL = OWN + 4 * GHOST
TRASH = ALL
PAIRS = 512
NX, NY = 8, 32
GROUP = 8
KDIM = 96
ROWS = 9 * GHOST

strength = 0.2
core_sq = 0.05
far_gain = 0.5
far_core_sq = 0.1


def mm(a, b, nt=False):
    dims = (((1,), (1 if nt else 0,)), ((), ()))
    return lax.dot_general(a, b, dims, preferred_element_type=f32)


def split3(x):
    h = x.astype(bf16)
    r = x - h.astype(f32)
    m = r.astype(bf16)
    return h, m, (r - m.astype(f32)).astype(bf16)


def rows16(parts):
    missing = 16 - sum(p.shape[0] for p in parts)
    if missing:
        parts = parts + [jnp.zeros((missing, BLOCK), f32)]
    return jnp.concatenate(parts, axis=0)


def eye128():
    shape = (BLOCK, BLOCK)
    return (lax.broadcasted_iota(i32, shape, 0) == lax.broadcasted_iota(i32, shape, 1)).astype(bf16)


def neighbours(ix, iy):
    return (
        (lax.rem(ix + NX - 1, NX), iy),
        (lax.rem(ix + 1, NX), iy),
        (ix, lax.rem(iy + NY - 1, NY)),
        (ix, lax.rem(iy + 1, NY)),
    )


def exchange(send_list, seg, cells, ghost_out, mom_out, main, last, out_buf, in_buf, row, part, row2, table,
             s_sem, r_sem, s1, r1, s2, r2):
    ix, iy = lax.axis_index("gx"), lax.axis_index("gy")
    barrier = pltpu.get_barrier_semaphore()

    def greet_y(o, _):
        pl.semaphore_signal(barrier, inc=1, device_id=(ix, lax.rem(iy + o, NY)), device_id_type=MESH)
        return 0

    def greet_x(o, _):
        pl.semaphore_signal(barrier, inc=1, device_id=(lax.rem(ix + o, NX), iy), device_id_type=MESH)
        return 0

    lax.fori_loop(1, NY, greet_y, 0)
    lax.fori_loop(1, NX, greet_x, 0)
    for k in range(OWN):
        main[k] = seg[0:8, k * BLOCK : (k + 1) * BLOCK]
        last[k] = seg[8:9, k * BLOCK : (k + 1) * BLOCK]
    for q in range(4):
        for j in range(GHOST):
            k = send_list[q, j]
            out_buf[q, 8 * j : 8 * j + 8, :] = main[k]
            out_buf[q, 8 * GHOST + j : 8 * GHOST + j + 1, :] = last[k]
    c = jnp.sum(seg[3:6, :] * seg[6:9, :], axis=0, keepdims=True)
    first = 2 * (ix * NY + iy)
    ids = cells[...]
    m0 = jnp.sum(jnp.where(ids == first, c, 0.0))
    m1 = jnp.sum(jnp.where(ids == first + 1, c, 0.0))
    lane = lax.broadcasted_iota(i32, (1, BLOCK), 1)
    mine = jnp.where(lane == 2 * iy, m0, jnp.where(lane == 2 * iy + 1, m1, 0.0))
    row[...] = mine
    part[NY - 1 : NY, :] = mine
    pl.semaphore_wait(barrier, NY - 1 + NX - 1)
    copies = []
    for q, dev in enumerate(neighbours(ix, iy)):
        copies.append(
            pltpu.make_async_remote_copy(
                src_ref=out_buf.at[q], dst_ref=in_buf.at[q ^ 1], send_sem=s_sem.at[q],
                recv_sem=r_sem.at[q ^ 1], device_id=dev, device_id_type=MESH,
            )
        )
        copies[-1].start()

    def send_y(o, _):
        pltpu.make_async_remote_copy(
            src_ref=row, dst_ref=part.at[pl.ds(o - 1, 1)], send_sem=s1, recv_sem=r1,
            device_id=(ix, lax.rem(iy + o, NY)), device_id_type=MESH,
        ).start()
        return 0

    lax.fori_loop(1, NY, send_y, 0)
    pltpu.make_async_copy(part.at[0 : NY - 1], part.at[0 : NY - 1], r1).wait()
    slab = jnp.sum(part[...], axis=0, keepdims=True)
    row2[...] = slab
    table[pl.ds(NX - 1, 1), :] = slab

    def send_x(o, _):
        pltpu.make_async_remote_copy(
            src_ref=row2, dst_ref=table.at[pl.ds(o - 1, 1)], send_sem=s2, recv_sem=r2,
            device_id=(lax.rem(ix + o, NX), iy), device_id_type=MESH,
        ).start()
        return 0

    lax.fori_loop(1, NX, send_x, 0)
    for cp in copies:
        cp.wait()
    ghost_out[...] = in_buf[...]
    pltpu.make_async_copy(table.at[0 : NX - 1], table.at[0 : NX - 1], r2).wait()
    mom_out[...] = table[...]
    pltpu.make_async_copy(part.at[0 : NY - 1], part.at[0 : NY - 1], s1).wait()
    pltpu.make_async_copy(table.at[0 : NX - 1], table.at[0 : NX - 1], s2).wait()


def features(raw, cx, cy, eye, a_ref, b_ref, p_ref, k, with_a):
    x, y, z = raw[0:1] - cx, raw[1:2] - cy, raw[2:3] - 0.5
    l, b = raw[3:6], raw[6:9]
    u = [b[0:1] * l, b[1:2] * l, b[2:3] * l]
    norm = x * x + y * y + z * z
    one = jnp.ones((1, BLOCK), f32)
    bq = split3(rows16(u))
    bd = split3(rows16([jnp.zeros((9, BLOCK), f32), x, y, z, norm, one]))
    order = (0, 1, 0, 1, 2, 0)
    b_ref[k, :, 0:BLOCK] = jnp.concatenate([bq[o] for o in order], axis=0)
    b_ref[k, :, BLOCK:] = jnp.concatenate([bd[o] for o in order], axis=0)
    pos = [t.astype(f32) for t in split3(x) + split3(y) + split3(z)]
    px = rows16(pos + [one]).astype(bf16)
    p_ref[k] = jnp.concatenate([px, px], axis=1)
    if with_a:
        fa = split3(
            rows16([strength * t for t in u] + [-2.0 * x, -2.0 * y, -2.0 * z, one, norm + core_sq])
        )
        at = jnp.concatenate([fa[o] for o in (0, 0, 1, 1, 0, 2)], axis=0)
        at = jnp.concatenate([at, jnp.zeros((BLOCK - KDIM, BLOCK), bf16)], axis=0)
        a_ref[k] = mm(eye, at, nt=True).astype(bf16)


def finish(acc, x, y, z):
    s = acc[9:10]
    return jnp.concatenate(
        [
            x * s - (acc[0:1] + acc[1:2] + acc[2:3]),
            y * s - (acc[3:4] + acc[4:5] + acc[5:6]),
            z * s - (acc[6:7] + acc[7:8] + acc[8:9]),
        ],
        axis=0,
    )


def pairs(count, rows, send_list, seg, ghost, own_out, ghost_out, inv_out, a_ref, b_ref, p_ref,
          qd, ww, rr, acc_a, acc_b):
    ix, iy = lax.axis_index("gx"), lax.axis_index("gy")
    cx, cy = ix.astype(f32) + 0.5, iy.astype(f32) + 0.5
    eye = eye128()

    def own_block(k):
        return seg[:, pl.ds(pl.multiple_of(k * BLOCK, BLOCK), BLOCK)]

    def ghost_block(q, j):
        return jnp.concatenate(
            [ghost[q, pl.ds(pl.multiple_of(8 * j, 8), 8), :], ghost[q, pl.ds(8 * GHOST + j, 1), :]], axis=0
        )

    def build_own(k, _):
        features(own_block(k), cx, cy, eye, a_ref, b_ref, p_ref, k, True)
        return 0

    def build_ghost(j, _):
        for q in range(4):
            features(ghost_block(q, j), cx, cy, eye, a_ref, b_ref, p_ref, OWN + GHOST * q + j, False)
        return 0

    lax.fori_loop(0, OWN, build_own, 0, unroll=4)
    lax.fori_loop(0, GHOST, build_ghost, 0)
    for acc in (acc_a, acc_b):
        acc[...] = jnp.zeros_like(acc)

    def step(t, _):
        for s in range(GROUP):
            o = t * (4 * GROUP) + 4 * s
            acc_a[rows[o + 2]] += rr[s, 0]
            acc_b[rows[o + 3]] += rr[s, 1]
            o = o + 4 * GROUP
            rr[s, 0] = mm(p_ref[rows[o + 1]], jnp.concatenate([ww[s, 0:BLOCK], ww[s, BLOCK:]], axis=1), nt=True)
            rr[s, 1] = mm(p_ref[rows[o]], ww[s])
            r = lax.rsqrt(qd[s, :, BLOCK:])
            w = (qd[s, :, 0:BLOCK] * r) * (r * r)
            wh = w.astype(bf16)
            ww[s, 0:BLOCK] = wh
            ww[s, BLOCK:] = (w - wh.astype(f32)).astype(bf16)
            o = o + 8 * GROUP
            qd[s] = mm(a_ref[rows[o], :, 0:KDIM], b_ref[rows[o + 1]])
        return 0

    lax.fori_loop(0, (count[0] + OWN + GROUP - 1) // GROUP + 3, step, 0)

    def finish_own(k, _):
        raw = own_block(k)
        own_out[k] = finish(acc_a[k] + acc_b[k], raw[0:1] - cx, raw[1:2] - cy, raw[2:3] - 0.5)
        return 0

    def finish_ghost(j, _):
        for q in range(4):
            raw = ghost_block(q, j)
            f = finish(acc_b[OWN + GHOST * q + j], raw[0:1] - cx, raw[1:2] - cy, raw[2:3] - 0.5)
            ghost_out[q, j] = jnp.concatenate([f, jnp.zeros((1, BLOCK), f32)], axis=0)
        return 0

    lax.fori_loop(0, OWN, finish_own, 0, unroll=4)
    lax.fori_loop(0, GHOST, finish_ghost, 0)

    def clear(k, _):
        for q in range(4):
            inv_out[q, k] = GHOST
        return 0

    lax.fori_loop(0, OWN, clear, 0, unroll=8)
    for q in range(4):
        for j in range(GHOST):
            inv_out[q, send_list[q, j]] = j


def finale(inv, seg, mom, own, ghost, out, back_in, mb, s_sem, r_sem):
    ix, iy = lax.axis_index("gx"), lax.axis_index("gy")
    barrier = pltpu.get_barrier_semaphore()
    near = neighbours(ix, iy)
    for dev in near:
        pl.semaphore_signal(barrier, inc=1, device_id=dev, device_id_type=MESH)
    wide = jnp.concatenate([mom[...], jnp.zeros((BLOCK - NX, BLOCK), f32)], axis=0).T
    for s in range(NX):
        mb[s] = jnp.broadcast_to(wide[0 : 2 * NY, s : s + 1], (2 * NY, BLOCK))
    pl.semaphore_wait(barrier, 4)
    copies = []
    for q, dev in enumerate(near):
        copies.append(
            pltpu.make_async_remote_copy(
                src_ref=ghost.at[q], dst_ref=back_in.at[q ^ 1, 0:GHOST], send_sem=s_sem.at[q],
                recv_sem=r_sem.at[q ^ 1], device_id=dev, device_id_type=MESH,
            )
        )
        copies[-1].start()
    for q in range(4):
        back_in[q, GHOST] = jnp.zeros((4, BLOCK), f32)
    groups = 2 * NY // 8
    sub = lax.broadcasted_iota(i32, (8, BLOCK), 0).astype(f32)
    centre_x = []
    for s in range(NX):
        src = lax.rem(ix + (2 * NX - 1 - s), NX)
        centre_x.append(src.astype(f32) + 0.5)

    def far(k, _):
        blk = seg[:, pl.ds(pl.multiple_of(k * BLOCK, BLOCK), BLOCK)]
        x, y, z = blk[0:1], blk[1:2], blk[2:3] - 0.5
        wide_y = jnp.broadcast_to(y, (8, BLOCK))
        base = z * z + far_core_sq
        dx = [jnp.broadcast_to(x - cx, (8, BLOCK)) for cx in centre_x]
        dx2 = [d * d for d in dx]
        hx = [None] * NX
        fy = total = None
        for g in range(groups):
            dy = wide_y - (0.5 * sub + (4.0 * g + 0.25))
            by = dy * dy + base
            gy = None
            for s in range(NX):
                r = lax.rsqrt(by + dx2[s])
                w = (mb[s, 8 * g : 8 * g + 8, :] * r) * (r * r)
                hx[s] = w if hx[s] is None else hx[s] + w
                gy = w if gy is None else gy + w
            total = gy if total is None else total + gy
            fy = dy * gy if fy is None else fy + dy * gy
        fx = dx[0] * hx[0]
        for s in range(1, NX):
            fx = fx + dx[s] * hx[s]
        weight = far_gain * jnp.sum(blk[3:6] * blk[6:9], axis=0, keepdims=True)
        add = lambda t: jnp.sum(t, axis=0, keepdims=True)
        f = jnp.concatenate([add(fx), add(fy), z * add(total)], axis=0)
        out[:, pl.ds(pl.multiple_of(k * BLOCK, BLOCK), BLOCK)] = own[k] + weight * f
        return 0

    lax.fori_loop(0, OWN, far, 0)
    for cp in copies:
        cp.wait()

    def combine(k, _):
        f = back_in[0, inv[0, k]]
        for q in range(1, 4):
            f = f + back_in[q, inv[q, k]]
        where = pl.ds(pl.multiple_of(k * BLOCK, BLOCK), BLOCK)
        out[:, where] = out[:, where] + f[0:3]
        return 0

    lax.fori_loop(0, OWN, combine, 0, unroll=4)


def index_rows(pair_list, pair_count):
    live = (jnp.arange(PAIRS, dtype=i32) < pair_count[0])[:, None]
    own = jnp.arange(OWN, dtype=i32)
    idle = jnp.array([[0, 0, TRASH, TRASH]], i32)
    pad = lambda n: jnp.broadcast_to(idle, (n, 4))
    self_rows = jnp.stack([own, own, jnp.full((OWN,), TRASH, i32), own], axis=1)
    pair_rows = jnp.where(live, jnp.concatenate([pair_list, pair_list], axis=1), idle)
    return jnp.concatenate([pad(3 * GROUP), self_rows, pair_rows, pad(5 * GROUP)], axis=0).reshape(-1)


VM, SM = pl.BlockSpec(memory_space=pltpu.VMEM), pl.BlockSpec(memory_space=pltpu.SMEM)
SDS = jax.ShapeDtypeStruct
DMA = pltpu.SemaphoreType.DMA


def body(segments, pair_list, pair_count, send_list, cell_ids):
    ghost, mom = pl.pallas_call(
        exchange,
        name="exchange",
        out_shape=(SDS((4, ROWS, BLOCK), f32), SDS((NX, BLOCK), f32)),
        in_specs=[SM, VM, VM],
        out_specs=(VM, VM),
        scratch_shapes=[
            pltpu.VMEM((OWN, 8, BLOCK), f32),
            pltpu.VMEM((OWN, 1, BLOCK), f32),
            pltpu.VMEM((4, ROWS, BLOCK), f32),
            pltpu.VMEM((4, ROWS, BLOCK), f32),
            pltpu.VMEM((1, BLOCK), f32),
            pltpu.VMEM((NY, BLOCK), f32),
            pltpu.VMEM((1, BLOCK), f32),
            pltpu.VMEM((NX, BLOCK), f32),
            DMA((4,)), DMA((4,)), DMA, DMA, DMA, DMA,
        ],
        compiler_params=pltpu.CompilerParams(
            collective_id=0, has_side_effects=True, vmem_limit_bytes=32 * 2**20
        ),
    )(send_list, segments, cell_ids.reshape(1, -1))
    own_force, ghost_force, inv = pl.pallas_call(
        pairs,
        name="pairs",
        out_shape=(SDS((OWN, 3, BLOCK), f32), SDS((4, GHOST, 4, BLOCK), f32), SDS((4, OWN), i32)),
        in_specs=[SM, SM, SM, VM, VM],
        out_specs=(VM, VM, SM),
        scratch_shapes=[
            pltpu.VMEM((OWN, BLOCK, BLOCK), bf16),
            pltpu.VMEM((ALL, KDIM, 2 * BLOCK), bf16),
            pltpu.VMEM((ALL, 16, 2 * BLOCK), bf16),
            pltpu.VMEM((GROUP, BLOCK, 2 * BLOCK), f32),
            pltpu.VMEM((GROUP, 2 * BLOCK, BLOCK), bf16),
            pltpu.VMEM((GROUP, 2, 16, BLOCK), f32),
            pltpu.VMEM((ALL + 1, 16, BLOCK), f32),
            pltpu.VMEM((ALL + 1, 16, BLOCK), f32),
        ],
        compiler_params=pltpu.CompilerParams(vmem_limit_bytes=40 * 2**20),
    )(pair_count, index_rows(pair_list, pair_count), send_list, segments, ghost)
    return pl.pallas_call(
        finale,
        name="finale",
        out_shape=SDS((3, OWN * BLOCK), f32),
        in_specs=[SM, VM, VM, VM, VM],
        out_specs=VM,
        scratch_shapes=[
            pltpu.VMEM((4, GHOST + 1, 4, BLOCK), f32),
            pltpu.VMEM((NX, 2 * NY, BLOCK), f32),
            DMA((4,)), DMA((4,)),
        ],
        compiler_params=pltpu.CompilerParams(
            collective_id=1, has_side_effects=True, vmem_limit_bytes=32 * 2**20
        ),
    )(inv, segments, mom, own_force, ghost_force)


def solution(mesh):
    in_specs = (
        P(None, ("gx", "gy")),
        P(("gx", "gy"), None),
        P(("gx", "gy")),
        P(("gx", "gy"), None),
        P(("gx", "gy")),
    )
    out_specs = P(None, ("gx", "gy"))
    return jax.shard_map(body, mesh=mesh, in_specs=in_specs, out_specs=out_specs, check_vma=False)
```

time: 552 us -> 67.6 us (0.12)
  the two profiles are of different devices: /device:TPU:75 before, /device:TPU:225 now
where the time goes in v1:
time: 67.6 us; the launch traced here: 67.5 us
  Pallas kernels  64.8 us (96%)
  local copies, waits for them, and re-layouts  1.73 us (3%)
  between operations  0.8 us (1%)
    pallas_call x1, Pallas kernels, body(): pl.pallas_call(finale, name='finale', out_shape=SDS((3, OWN * BLOCK), f32...  25.9 us
    pallas_call x1, Pallas kernels, body(): pl.pallas_call(pairs, name='pairs', out_shape=(SDS((OWN, 3, BLOCK), f32),...  23.3 us
    pallas_call x1, Pallas kernels, body(): pl.pallas_call(exchange, name='exchange', out_shape=(SDS((4, ROWS, BLOCK)...  15.6 us

profile of v1, /device:TPU:225, one launch (start us, length us, event | category | flops | bytes accessed | tf_op | source)
XLA Modules:
  0.0 67.5 jit_solution(2358592174979847634)
XLA Ops:
  0.0 0.0 copy-start.3
  0.0 0.0 copy-start.4
  0.0 0.0 copy-start
  0.7 0.0 copy-done.3
  0.7 0.0 copy-done.4
  0.8 0.1 add_select_fusion
  0.8 0.1 broadcast_in_dim.30
  0.9 0.1 broadcast_in_dim.33
  1.0 0.1 pad_add_fusion
  1.0 0.2 copy.7
  1.2 0.0 copy-start.1
  1.2 0.0 copy-start.2
  1.3 0.2 reshape.10.rows
  1.5 0.0 copy-done
  1.5 0.5 copy-done.1
  2.0 0.0 copy-done.2
  2.0 15.6 %exchange.1 = (f32[4,144,128]{2,1,0:T(8,128)S(1)}, f32[8,128]{1,0:T(8,128)S(1)}) custom-call(s32[4,16]{1,0:T(4,128)S(1)} %copy-done.2, f32[9,8192]{1,0:T(8,128)S(1)} %copy-done, s32[1,8192]{1,0:T(1,128)S(1)} %bitcast.3), custom_call_target="tpu_custom_call" | custom-call | tf_op jit(solution)/shard_map/exchange/pallas_call | solution.py:331
  17.6 23.3 %pairs.1 = (f32[64,3,128]{2,1,0:T(4,128)S(1)}, f32[4,16,4,128]{3,2,1,0:T(4,128)S(1)}, s32[4,64]{1,0:T(4,128)S(1)}) custom-call(s32[1]{0:T(128)} %copy.9.count, s32[2560]{0:T(1024)S(1)} %reshape.10.rows, s32[4,16]{1,0:T(4,128)S(1)} %copy-done.2, f32[9,8192]{1,0:T(8,128)S(1)} %copy-done, f32[4,144,128]{2,1,0:T(8,128)S(1)} %get-tuple-element.10.ghost), custom_call_target="tpu_custom_call" | custom-call | tf_op jit(solution)/shard_map/pairs/pallas_call | solution.py:352
  40.9 25.9 %finale.1 = f32[3,8192]{1,0:T(4,128)S(1)} custom-call(s32[4,64]{1,0:T(4,128)S(1)} %get-tuple-element.11.inv, f32[9,8192]{1,0:T(8,128)S(1)} %copy-done, f32[8,128]{1,0:T(8,128)S(1)} %get-tuple-element.12.mom, f32[64,3,128]{2,1,0:T(4,128)S(1)} %get-tuple-element.13.own, f32[4,16,4,128]{3,2,1,0:T(4,128)S(1)} %get-tuple-element.14.ghost), custom_call_target="tpu_custom_call" | custom-call | tf_op jit(solution)/shard_map/finale/pallas_call | solution.py:370
  66.8 0.7 copy.10
  (3 shorter events, 0.0 us)
Async XLA Ops:
  0.0 0.7 %copy-start.3 = (s32[4]{0:T(128)S(1)}, s32[4]{0:T(128)}, u32[]{:S(2)}) copy-start(s32[4]{0:T(128)} %constant.7) | copy-start | bytes 52
  0.0 0.7 %copy-start.4 = (s32[512,2]{0,1:T(2,128)S(1)}, s32[512,2]{0,1:T(2,128)}, u32[]{:S(2)}) copy-start(s32[512,2]{0,1:T(2,128)} %param.7) | copy-start | bytes 12292
  0.0 1.5 %copy-start = (f32[9,8192]{1,0:T(8,128)S(1)}, f32[9,8192]{1,0:T(8,128)}, u32[]{:S(2)}) copy-start(f32[9,8192]{1,0:T(8,128)} %seg.5) | copy-start | bytes 884740
  1.2 0.8 %copy-start.1 = (s32[8192]{0:T(1024)S(1)}, s32[8192]{0:T(1024)}, u32[]{:S(2)}) copy-start(s32[8192]{0:T(1024)} %param.10) | copy-start | bytes 98308
  1.2 0.8 %copy-start.2 = (s32[4,16]{1,0:T(4,128)S(1)}, s32[4,16]{1,0:T(4,128)}, u32[]{:S(2)}) copy-start(s32[4,16]{1,0:T(4,128)} %send_list.3) | copy-start | bytes 772

commit v2 on v1

v2 whole, which is shorter than its diff:
```python
import functools

import jax
import jax.numpy as jnp
from jax import lax
from jax.experimental import pallas as pl
from jax.experimental.pallas import tpu as pltpu
from jax.sharding import PartitionSpec as P

f32, bf16, i32 = jnp.float32, jnp.bfloat16, jnp.int32
MESH = pl.DeviceIdType.MESH
BLOCK = 128
OWN = 64
GHOST = 16
ALL = OWN + 4 * GHOST
TRASH = ALL
PAIRS = 512
NX, NY = 8, 32
GROUP = 8
KDIM = 96
ROWS = 9 * GHOST

strength = 0.2
core_sq = 0.05
far_gain = 0.5
far_core_sq = 0.1


def mm(a, b, nt=False):
    dims = (((1,), (1 if nt else 0,)), ((), ()))
    return lax.dot_general(a, b, dims, preferred_element_type=f32)


def split3(x):
    h = x.astype(bf16)
    r = x - h.astype(f32)
    m = r.astype(bf16)
    return h, m, (r - m.astype(f32)).astype(bf16)


def rows16(parts):
    missing = 16 - sum(p.shape[0] for p in parts)
    if missing:
        parts = parts + [jnp.zeros((missing, BLOCK), f32)]
    return jnp.concatenate(parts, axis=0)


def eye128():
    shape = (BLOCK, BLOCK)
    return (lax.broadcasted_iota(i32, shape, 0) == lax.broadcasted_iota(i32, shape, 1)).astype(bf16)


def neighbours(ix, iy):
    return (
        (lax.rem(ix + NX - 1, NX), iy),
        (lax.rem(ix + 1, NX), iy),
        (ix, lax.rem(iy + NY - 1, NY)),
        (ix, lax.rem(iy + 1, NY)),
    )


def features(raw, cx, cy, eye, a_ref, b_ref, p_ref, k, with_a):
    x, y, z = raw[0:1] - cx, raw[1:2] - cy, raw[2:3] - 0.5
    l, b = raw[3:6], raw[6:9]
    u = [b[0:1] * l, b[1:2] * l, b[2:3] * l]
    norm = x * x + y * y + z * z
    one = jnp.ones((1, BLOCK), f32)
    bq = split3(rows16(u))
    bd = split3(rows16([jnp.zeros((9, BLOCK), f32), x, y, z, norm, one]))
    b_ref[k, :, 0:BLOCK] = jnp.concatenate(bq, axis=0)
    b_ref[k, :, BLOCK:] = jnp.concatenate(bd, axis=0)
    pos = [t.astype(f32) for t in split3(x) + split3(y) + split3(z)]
    p_ref[k] = rows16(pos + [one]).astype(bf16)
    if with_a:
        fa = split3(
            rows16([strength * t for t in u] + [-2.0 * x, -2.0 * y, -2.0 * z, one, norm + core_sq])
        )
        at = jnp.concatenate([fa[o] for o in (0, 0, 1, 1, 0, 2)], axis=0)
        at = jnp.concatenate([at, jnp.zeros((BLOCK - KDIM, BLOCK), bf16)], axis=0)
        a_ref[k] = mm(eye, at, nt=True).astype(bf16)


def twice(p):
    return jnp.concatenate([p, p], axis=1)


def spread(b):
    h, m, l = b[0:16], b[16:32], b[32:48]
    return jnp.concatenate([h, m, h, m, l, h], axis=0)


def twice_w(ww, s):
    return jnp.concatenate([ww[s, 0:BLOCK], ww[s, BLOCK:]], axis=1)


def weigh(qd, ww, s):
    r = lax.rsqrt(qd[s, :, BLOCK:])
    w = (qd[s, :, 0:BLOCK] * r) * (r * r)
    wh = w.astype(bf16)
    ww[s, 0:BLOCK] = wh
    ww[s, BLOCK:] = (w - wh.astype(f32)).astype(bf16)


def exchange(send_list, seg, cells, a_ref, b_ref, p_ref, self_ref, mom_out, main, last, out_buf, in_buf,
             row, part, row2, table, qd, ww, s_sem, r_sem, s1, r1, s2, r2):
    ix, iy = lax.axis_index("gx"), lax.axis_index("gy")
    barrier = pltpu.get_barrier_semaphore()

    def greet_y(o, _):
        pl.semaphore_signal(barrier, inc=1, device_id=(ix, lax.rem(iy + o, NY)), device_id_type=MESH)
        return 0

    def greet_x(o, _):
        pl.semaphore_signal(barrier, inc=1, device_id=(lax.rem(ix + o, NX), iy), device_id_type=MESH)
        return 0

    lax.fori_loop(1, NY, greet_y, 0)
    lax.fori_loop(1, NX, greet_x, 0)
    for k in range(OWN):
        main[k] = seg[0:8, k * BLOCK : (k + 1) * BLOCK]
        last[k] = seg[8:9, k * BLOCK : (k + 1) * BLOCK]
    for q in range(4):
        for j in range(GHOST):
            k = send_list[q, j]
            out_buf[q, 8 * j : 8 * j + 8, :] = main[k]
            out_buf[q, 8 * GHOST + j : 8 * GHOST + j + 1, :] = last[k]
    c = jnp.sum(seg[3:6, :] * seg[6:9, :], axis=0, keepdims=True)
    first = 2 * (ix * NY + iy)
    ids = cells[...]
    m0 = jnp.sum(jnp.where(ids == first, c, 0.0))
    m1 = jnp.sum(jnp.where(ids == first + 1, c, 0.0))
    lane = lax.broadcasted_iota(i32, (1, BLOCK), 1)
    mine = jnp.where(lane == 2 * iy, m0, jnp.where(lane == 2 * iy + 1, m1, 0.0))
    row[...] = mine
    part[NY - 1 : NY, :] = mine
    pl.semaphore_wait(barrier, NY - 1 + NX - 1)
    copies = []
    for q, dev in enumerate(neighbours(ix, iy)):
        copies.append(
            pltpu.make_async_remote_copy(
                src_ref=out_buf.at[q], dst_ref=in_buf.at[q ^ 1], send_sem=s_sem.at[q],
                recv_sem=r_sem.at[q ^ 1], device_id=dev, device_id_type=MESH,
            )
        )
        copies[-1].start()

    def send_y(o, _):
        pltpu.make_async_remote_copy(
            src_ref=row, dst_ref=part.at[pl.ds(o - 1, 1)], send_sem=s1, recv_sem=r1,
            device_id=(ix, lax.rem(iy + o, NY)), device_id_type=MESH,
        ).start()
        return 0

    lax.fori_loop(1, NY, send_y, 0)
    cx, cy = ix.astype(f32) + 0.5, iy.astype(f32) + 0.5
    eye = eye128()

    def build_own(k, _):
        raw = jnp.concatenate([main[k], last[k]], axis=0)
        features(raw, cx, cy, eye, a_ref, b_ref, p_ref, k, True)
        return 0

    lax.fori_loop(0, OWN, build_own, 0, unroll=4)
    pltpu.make_async_copy(part.at[0 : NY - 1], part.at[0 : NY - 1], r1).wait()
    slab = jnp.sum(part[...], axis=0, keepdims=True)
    row2[...] = slab
    table[pl.ds(NX - 1, 1), :] = slab

    def send_x(o, _):
        pltpu.make_async_remote_copy(
            src_ref=row2, dst_ref=table.at[pl.ds(o - 1, 1)], send_sem=s2, recv_sem=r2,
            device_id=(lax.rem(ix + o, NX), iy), device_id_type=MESH,
        ).start()
        return 0

    lax.fori_loop(1, NX, send_x, 0)

    def step(t, _):
        for s in range(GROUP):
            k = (t - 2) * GROUP + s
            k = jnp.minimum(jnp.maximum(k, 0), OWN - 1)
            self_ref[k] = mm(twice(p_ref[k]), ww[s])
            weigh(qd, ww, s)
            k = jnp.minimum(t * GROUP + s, OWN - 1)
            qd[s] = mm(a_ref[k, :, 0:KDIM], spread(b_ref[k]))
        return 0

    lax.fori_loop(0, OWN // GROUP + 2, step, 0)
    for cp in copies:
        cp.wait()

    def build_ghost(j, _):
        for q in range(4):
            raw = jnp.concatenate(
                [in_buf[q, pl.ds(pl.multiple_of(8 * j, 8), 8), :], in_buf[q, pl.ds(8 * GHOST + j, 1), :]], axis=0
            )
            features(raw, cx, cy, eye, a_ref, b_ref, p_ref, OWN + GHOST * q + j, False)
        return 0

    lax.fori_loop(0, GHOST, build_ghost, 0)
    pltpu.make_async_copy(table.at[0 : NX - 1], table.at[0 : NX - 1], r2).wait()
    mom_out[...] = table[...]
    pltpu.make_async_copy(part.at[0 : NY - 1], part.at[0 : NY - 1], s1).wait()
    pltpu.make_async_copy(table.at[0 : NX - 1], table.at[0 : NX - 1], s2).wait()


def finish(acc, p):
    p = p.astype(f32)
    f = []
    for c in range(3):
        x = p[3 * c : 3 * c + 1] + p[3 * c + 1 : 3 * c + 2] + p[3 * c + 2 : 3 * c + 3]
        f.append(x * acc[9:10] - (acc[3 * c : 3 * c + 1] + acc[3 * c + 1 : 3 * c + 2] + acc[3 * c + 2 : 3 * c + 3]))
    return f


def pairs(count, rows, send_list, seg, mom, a_ref, b_ref, p_ref, self_ref, own_out, ghost_out, inv_out,
          qd, ww, rr, acc_a, acc_b, mb, far_out):
    ix = lax.axis_index("gx")
    acc_a[...] = jnp.zeros_like(acc_a)
    acc_b[0:OWN] = self_ref[...]
    acc_b[OWN:] = jnp.zeros((ALL + 1 - OWN, 16, BLOCK), f32)
    wide = jnp.concatenate([mom[...], jnp.zeros((BLOCK - NX, BLOCK), f32)], axis=0).T
    for s in range(NX):
        mb[s] = jnp.broadcast_to(wide[0 : 2 * NY, s : s + 1], (2 * NY, BLOCK))
    centre_x = [lax.rem(ix + (2 * NX - 1 - s), NX).astype(f32) + 0.5 for s in range(NX)]
    sub = lax.broadcasted_iota(i32, (8, BLOCK), 0).astype(f32)

    class Far:
        def __init__(self, k):
            self.k = k
            blk = seg[:, pl.ds(pl.multiple_of(jnp.minimum(k, OWN - 1) * BLOCK, BLOCK), BLOCK)]
            self.blk = blk
            self.y = jnp.broadcast_to(blk[1:2], (8, BLOCK))
            z = blk[2:3] - 0.5
            self.base = z * z + far_core_sq
            x = jnp.broadcast_to(blk[0:1], (8, BLOCK))
            self.dx2 = [(x - cx) * (x - cx) for cx in centre_x]
            self.hx, self.fy, self.total = [None] * NX, None, None

        def group(self, g):
            dy = self.y - (0.5 * sub + (4.0 * g + 0.25))
            by = dy * dy + self.base
            gy = None
            for s in range(NX):
                r = lax.rsqrt(by + self.dx2[s])
                w = (mb[s, 8 * g : 8 * g + 8, :] * r) * (r * r)
                self.hx[s] = w if g == 0 else self.hx[s] + w
                gy = w if gy is None else gy + w
            self.total = gy if g == 0 else self.total + gy
            self.fy = dy * gy if g == 0 else self.fy + dy * gy

        def store(self):
            blk = self.blk
            x = jnp.broadcast_to(blk[0:1], (8, BLOCK))
            fx = (x - centre_x[0]) * self.hx[0]
            for s in range(1, NX):
                fx = fx + (x - centre_x[s]) * self.hx[s]
            weight = far_gain * jnp.sum(blk[3:6] * blk[6:9], axis=0, keepdims=True)
            add = lambda t: jnp.sum(t, axis=0, keepdims=True)
            f = jnp.concatenate([add(fx), add(self.fy), (blk[2:3] - 0.5) * add(self.total)], axis=0)
            far_out[self.k] = weight * f

    def step(t, _):
        far = Far(jnp.minimum(t, OWN))
        for s in range(GROUP):
            o = t * (4 * GROUP) + 4 * s
            acc_a[rows[o + 2]] += rr[s, 0]
            acc_b[rows[o + 3]] += rr[s, 1]
            o = o + 4 * GROUP
            rr[s, 0] = mm(twice(p_ref[rows[o + 1]]), twice_w(ww, s), nt=True)
            rr[s, 1] = mm(twice(p_ref[rows[o]]), ww[s])
            weigh(qd, ww, s)
            far.group(s)
            o = o + 8 * GROUP
            qd[s] = mm(a_ref[rows[o], :, 0:KDIM], spread(b_ref[rows[o + 1]]))
        far.store()
        return 0

    steps = (count[0] + GROUP - 1) // GROUP + 3
    lax.fori_loop(0, steps, step, 0)

    def rest(k, _):
        far = Far(k)
        for g in range(GROUP):
            far.group(g)
        far.store()
        return 0

    lax.fori_loop(jnp.minimum(steps, OWN), OWN, rest, 0)

    def finish_own(k, _):
        own_out[k] = jnp.concatenate(finish(acc_a[k] + acc_b[k], p_ref[k]), axis=0) + far_out[k]
        return 0

    def finish_ghost(k, _):
        f = finish(acc_b[OWN + k], p_ref[OWN + k])
        ghost_out[k] = jnp.concatenate(f + [jnp.zeros((1, BLOCK), f32)], axis=0)
        return 0

    lax.fori_loop(0, OWN, finish_own, 0, unroll=4)
    lax.fori_loop(0, 4 * GHOST, finish_ghost, 0, unroll=4)

    def clear(k, _):
        for q in range(4):
            inv_out[q, k] = GHOST
        return 0

    lax.fori_loop(0, OWN, clear, 0, unroll=8)
    for q in range(4):
        for j in range(GHOST):
            inv_out[q, send_list[q, j]] = j


def finale(inv, own, ghost, out, back_in, s_sem, r_sem):
    ix, iy = lax.axis_index("gx"), lax.axis_index("gy")
    barrier = pltpu.get_barrier_semaphore()
    near = neighbours(ix, iy)
    for dev in near:
        pl.semaphore_signal(barrier, inc=1, device_id=dev, device_id_type=MESH)
    pl.semaphore_wait(barrier, 4)
    copies = []
    for q, dev in enumerate(near):
        copies.append(
            pltpu.make_async_remote_copy(
                src_ref=ghost.at[GHOST * q : GHOST * q + GHOST], dst_ref=back_in.at[q ^ 1, 0:GHOST], send_sem=s_sem.at[q],
                recv_sem=r_sem.at[q ^ 1], device_id=dev, device_id_type=MESH,
            )
        )
        copies[-1].start()
    for q in range(4):
        back_in[q, GHOST] = jnp.zeros((4, BLOCK), f32)
    for cp in copies:
        cp.wait()

    def combine(k, _):
        f = back_in[0, inv[0, k]]
        for q in range(1, 4):
            f = f + back_in[q, inv[q, k]]
        where = pl.ds(pl.multiple_of(k * BLOCK, BLOCK), BLOCK)
        out[:, where] = own[k] + f[0:3]
        return 0

    lax.fori_loop(0, OWN, combine, 0, unroll=4)


def index_rows(pair_list, pair_count):
    live = (jnp.arange(PAIRS, dtype=i32) < pair_count[0])[:, None]
    idle = jnp.array([[0, 0, TRASH, TRASH]], i32)
    pad = lambda n: jnp.broadcast_to(idle, (n, 4))
    pair_rows = jnp.where(live, jnp.concatenate([pair_list, pair_list], axis=1), idle)
    return jnp.concatenate([pad(3 * GROUP), pair_rows, pad(5 * GROUP)], axis=0).reshape(-1)


VM, SM = pl.BlockSpec(memory_space=pltpu.VMEM), pl.BlockSpec(memory_space=pltpu.SMEM)
SDS = jax.ShapeDtypeStruct
DMA = pltpu.SemaphoreType.DMA


def body(segments, pair_list, pair_count, send_list, cell_ids):
    a, b, p, own_sums, mom = pl.pallas_call(
        exchange,
        name="exchange",
        out_shape=(
            SDS((OWN, BLOCK, BLOCK), bf16),
            SDS((ALL, 48, 2 * BLOCK), bf16),
            SDS((ALL, 16, BLOCK), bf16),
            SDS((OWN, 16, BLOCK), f32),
            SDS((NX, BLOCK), f32),
        ),
        in_specs=[SM, VM, VM],
        out_specs=(VM,) * 5,
        scratch_shapes=[
            pltpu.VMEM((OWN, 8, BLOCK), f32),
            pltpu.VMEM((OWN, 1, BLOCK), f32),
            pltpu.VMEM((4, ROWS, BLOCK), f32),
            pltpu.VMEM((4, ROWS, BLOCK), f32),
            pltpu.VMEM((1, BLOCK), f32),
            pltpu.VMEM((NY, BLOCK), f32),
            pltpu.VMEM((1, BLOCK), f32),
            pltpu.VMEM((NX, BLOCK), f32),
            pltpu.VMEM((GROUP, BLOCK, 2 * BLOCK), f32),
            pltpu.VMEM((GROUP, 2 * BLOCK, BLOCK), bf16),
            DMA((4,)), DMA((4,)), DMA, DMA, DMA, DMA,
        ],
        compiler_params=pltpu.CompilerParams(
            collective_id=0, has_side_effects=True, vmem_limit_bytes=20 * 2**20
        ),
    )(send_list, segments, cell_ids.reshape(1, -1))
    own_force, ghost_force, inv = pl.pallas_call(
        pairs,
        name="pairs",
        out_shape=(SDS((OWN, 3, BLOCK), f32), SDS((4 * GHOST, 4, BLOCK), f32), SDS((4, OWN), i32)),
        in_specs=[SM, SM, SM] + [VM] * 6,
        out_specs=(VM, VM, SM),
        scratch_shapes=[
            pltpu.VMEM((GROUP, BLOCK, 2 * BLOCK), f32),
            pltpu.VMEM((GROUP, 2 * BLOCK, BLOCK), bf16),
            pltpu.VMEM((GROUP, 2, 16, BLOCK), f32),
            pltpu.VMEM((ALL + 1, 16, BLOCK), f32),
            pltpu.VMEM((ALL + 1, 16, BLOCK), f32),
            pltpu.VMEM((NX, 2 * NY, BLOCK), f32),
            pltpu.VMEM((OWN + 1, 3, BLOCK), f32),
        ],
        compiler_params=pltpu.CompilerParams(vmem_limit_bytes=24 * 2**20),
    )(pair_count, index_rows(pair_list, pair_count), send_list, segments, mom, a, b, p, own_sums)
    return pl.pallas_call(
        finale,
        name="finale",
        out_shape=SDS((3, OWN * BLOCK), f32),
        in_specs=[SM, VM, VM],
        out_specs=VM,
        scratch_shapes=[pltpu.VMEM((4, GHOST + 1, 4, BLOCK), f32), DMA((4,)), DMA((4,))],
        compiler_params=pltpu.CompilerParams(
            collective_id=1, has_side_effects=True, vmem_limit_bytes=16 * 2**20
        ),
    )(inv, own_force, ghost_force)


def solution(mesh):
    in_specs = (
        P(None, ("gx", "gy")),
        P(("gx", "gy"), None),
        P(("gx", "gy")),
        P(("gx", "gy"), None),
        P(("gx", "gy")),
    )
    out_specs = P(None, ("gx", "gy"))
    return jax.shard_map(body, mesh=mesh, in_specs=in_specs, out_specs=out_specs, check_vma=False)
```

time: 67.6 us -> 67.7 us (level)
  the two profiles are of different devices: /device:TPU:225 before, /device:TPU:121 now
where the time goes in v2:
time: 67.7 us; the launch traced here: 67.4 us
  Pallas kernels  59.1 us (87%)
  local copies, waits for them, and re-layouts  6.64 us (10%)
  other arithmetic  0.92 us (1%)
  between operations  0.72 us (1%)
    pallas_call x1, Pallas kernels, body(): pl.pallas_call(finale, name='finale', out_shape=SDS((3, OWN * BLOCK), f32...  25 us
    pallas_call x1, Pallas kernels, body(): pl.pallas_call(pairs, name='pairs', out_shape=(SDS((OWN, 3, BLOCK), f32),...  17.7 us
    pallas_call x1, Pallas kernels, body(): pl.pallas_call(exchange, name='exchange', out_shape=(SDS((OWN, BLOCK, BLO...  16.4 us
    unnamed x11, local copies, waits for them, and re-layouts  4.85 us
    broadcast_in_dim x2, local copies, waits for them, and re-layouts, index_rows(): pad = lambda n: jnp.broadcast_to(idle, (n, 4))  1.45 us

profile of v2, /device:TPU:121, one launch (start us, length us, event | category | flops | bytes accessed | tf_op | source)
XLA Modules:
  0.0 67.4 jit_solution(14005440062354467603)
XLA Ops:
  0.7 0.8 %add_select_fusion = s32[512,4]{0,1:T(4,128)S(1)} fusion(s32[512,2]{0,1:T(2,128)} %param.7, s32[4]{0:T(128)} %constant.5, pred[512]{0:T(512)(128)(4,1)S(1)} %iota_compare_fusion), kind=kLoop, calls=%fused_computation.1 | loop fusion | flops 4096 | bytes 12816 | tf_op jit(solution)/shard_map/jit(_where)/select_n | solution.py:350
  1.5 0.7 %broadcast_in_dim.33 = s32[40,4]{0,1:T(4,128)S(1)} broadcast(s32[4]{0:T(128)} %constant.5), dimensions={1} | broadcast | bytes 656 | tf_op jit(solution)/shard_map/broadcast_in_dim | solution.py:349
  2.2 0.7 %broadcast_in_dim.30 = s32[24,4]{0,1:T(4,128)S(1)} broadcast(s32[4]{0:T(128)} %constant.5), dimensions={1} | broadcast | bytes 400 | tf_op jit(solution)/shard_map/broadcast_in_dim | solution.py:349
  3.0 0.1 pad_add_fusion
  3.0 0.2 copy.7
  3.2 0.2 reshape.10.rows
  3.4 0.0 copy-start
  3.4 1.0 %copy-done = f32[9,8192]{1,0:T(8,128)S(1)} copy-done((f32[9,8192]{1,0:T(8,128)S(1)}, f32[9,8192]{1,0:T(8,128)}, u32[]{:S(2)}) %copy-start) | copy-done | bytes 294936
  4.4 0.0 copy-start.2
  4.4 0.8 %copy-done.2 = s32[8192]{0:T(1024)S(1)} copy-done((s32[8192]{0:T(1024)S(1)}, s32[8192]{0:T(1024)}, u32[]{:S(2)}) %copy-start.2) | copy-done | bytes 32792
  5.2 0.0 copy-start.3
  5.2 0.7 %copy-done.3 = s32[4,16]{1,0:T(4,128)S(1)} copy-done((s32[4,16]{1,0:T(4,128)S(1)}, s32[4,16]{1,0:T(4,128)}, u32[]{:S(2)}) %copy-start.3) | copy-done | bytes 280
  5.9 16.4 %exchange.1 = (bf16[64,128,128]{2,1,0:T(8,128)(2,1)S(1)}, bf16[128,48,256]{2,1,0:T(8,128)(2,1)S(1)}, bf16[128,16,128]{2,1,0:T(8,128)(2,1)S(1)}, f32[64,16,128]{2,1,0:T(8,128)S(1)}, f32[8,128]{1,0:T(8,128)S(1)}) custom-call(s32[4,16]{1,0:T(4,128)S(1)} %copy-done.3, f32[9,8192]{1,0:T(8,128)S(1)} %copy-done, s32[1,8192]{1,0:T(1,128)S(1)} %bitcast.3), custom_call_target="tpu_custom_call" | custom-call | tf_op jit(solution)/shard_map/exchange/pallas_call | solution.py:360
  22.3 0.0 copy-start.1
  22.3 1.0 %copy-done.1 = f32[9,8192]{1,0:T(8,128)S(1)} copy-done((f32[9,8192]{1,0:T(8,128)S(1)}, f32[9,8192]{1,0:T(8,128)}, u32[]{:S(2)}) %copy-start.1) | copy-done | bytes 294936
  23.4 0.0 copy-start.4
  23.4 0.7 %copy-done.4 = s32[4,16]{1,0:T(4,128)S(1)} copy-done((s32[4,16]{1,0:T(4,128)S(1)}, s32[4,16]{1,0:T(4,128)}, u32[]{:S(2)}) %copy-start.4) | copy-done | bytes 280
  24.1 17.7 %pairs.1 = (f32[64,3,128]{2,1,0:T(4,128)S(1)}, f32[64,4,128]{2,1,0:T(4,128)S(1)}, s32[4,64]{1,0:T(4,128)S(1)}) custom-call(s32[1]{0:T(128)} %copy.9.count, s32[2304]{0:T(1024)S(1)} %reshape.10.rows, s32[4,16]{1,0:T(4,128)S(1)} %copy-done.4, f32[9,8192]{1,0:T(8,128)S(1)} %copy-done.1, f32[8,128]{1,0:T(8,128)S(1)} %get-tuple-element.13.mom, ...), custom_call_target="tpu_custom_call" | custom-call | tf_op jit(solution)/shard_map/pairs/pallas_call | solution.py:389
  41.8 25.0 %finale.1 = f32[3,8192]{1,0:T(4,128)S(1)} custom-call(s32[4,64]{1,0:T(4,128)S(1)} %get-tuple-element.18.inv, f32[64,3,128]{2,1,0:T(4,128)S(1)} %get-tuple-element.19.own, f32[64,4,128]{2,1,0:T(4,128)S(1)} %get-tuple-element.20.ghost), custom_call_target="tpu_custom_call" | custom-call | tf_op jit(solution)/shard_map/finale/pallas_call | solution.py:406
  66.7 0.7 copy.10
  (1 shorter events, 0.0 us)
Async XLA Ops:
  3.4 1.0 %copy-start = (f32[9,8192]{1,0:T(8,128)S(1)}, f32[9,8192]{1,0:T(8,128)}, u32[]{:S(2)}) copy-start(f32[9,8192]{1,0:T(8,128)} %seg.3) | copy-start | bytes 884740
  4.4 0.8 %copy-start.2 = (s32[8192]{0:T(1024)S(1)}, s32[8192]{0:T(1024)}, u32[]{:S(2)}) copy-start(s32[8192]{0:T(1024)} %param.10) | copy-start | bytes 98308
  5.2 0.7 %copy-start.3 = (s32[4,16]{1,0:T(4,128)S(1)}, s32[4,16]{1,0:T(4,128)}, u32[]{:S(2)}) copy-start(s32[4,16]{1,0:T(4,128)} %send_list.3) | copy-start | bytes 772
  22.3 1.0 %copy-start.1 = (f32[9,8192]{1,0:T(8,128)S(1)}, f32[9,8192]{1,0:T(8,128)}, u32[]{:S(2)}) copy-start(f32[9,8192]{1,0:T(8,128)} %seg.3) | copy-start | bytes 884740
  23.4 0.7 %copy-start.4 = (s32[4,16]{1,0:T(4,128)S(1)}, s32[4,16]{1,0:T(4,128)}, u32[]{:S(2)}) copy-start(s32[4,16]{1,0:T(4,128)} %send_list.3) | copy-start | bytes 772

commit v3 on v2

v3 whole, which is shorter than its diff:
```python
import functools

import jax
import jax.numpy as jnp
from jax import lax
from jax.experimental import pallas as pl
from jax.experimental.pallas import tpu as pltpu
from jax.sharding import PartitionSpec as P

f32, bf16, i32 = jnp.float32, jnp.bfloat16, jnp.int32
MESH = pl.DeviceIdType.MESH
BLOCK = 128
OWN = 64
GHOST = 16
ALL = OWN + 4 * GHOST
SIB = ALL
TRASH = 2 * ALL
SURE = 64
PAIRS = 512
NX, NY = 8, 32
GROUP = 8
KDIM = 96
ROWS = 9 * GHOST

strength = 0.2
core_sq = 0.05
far_gain = 0.5
far_core_sq = 0.1


def mm(a, b, nt=False):
    dims = (((1,), (1 if nt else 0,)), ((), ()))
    return lax.dot_general(a, b, dims, preferred_element_type=f32)


def split3(x):
    h = x.astype(bf16)
    r = x - h.astype(f32)
    m = r.astype(bf16)
    return h, m, (r - m.astype(f32)).astype(bf16)


def rows16(parts):
    missing = 16 - sum(p.shape[0] for p in parts)
    if missing:
        parts = parts + [jnp.zeros((missing, BLOCK), f32)]
    return jnp.concatenate(parts, axis=0)


def eye128():
    shape = (BLOCK, BLOCK)
    return (lax.broadcasted_iota(i32, shape, 0) == lax.broadcasted_iota(i32, shape, 1)).astype(bf16)


def neighbours(ix, iy):
    return (
        (lax.rem(ix + NX - 1, NX), iy),
        (lax.rem(ix + 1, NX), iy),
        (ix, lax.rem(iy + NY - 1, NY)),
        (ix, lax.rem(iy + 1, NY)),
    )


def features(raw, cx, cy, eye, a_ref, b_ref, p_ref, k, with_a):
    k = jnp.int32(k) if isinstance(k, int) else k
    x, y, z = raw[0:1] - cx, raw[1:2] - cy, raw[2:3] - 0.5
    l, b = raw[3:6], raw[6:9]
    u = [b[0:1] * l, b[1:2] * l, b[2:3] * l]
    norm = x * x + y * y + z * z
    one = jnp.ones((1, BLOCK), f32)
    bq = split3(rows16(u))
    bd = split3(rows16([jnp.zeros((9, BLOCK), f32), x, y, z, norm, one]))
    b_ref[k, :, 0:BLOCK] = jnp.concatenate(bq, axis=0)
    b_ref[k, :, BLOCK:] = jnp.concatenate(bd, axis=0)
    pos = [t.astype(f32) for t in split3(x) + split3(y) + split3(z)]
    p_ref[k] = rows16(pos + [one]).astype(bf16)
    if with_a:
        fa = split3(
            rows16([strength * t for t in u] + [-2.0 * x, -2.0 * y, -2.0 * z, one, norm + core_sq])
        )
        at = jnp.concatenate([fa[o] for o in (0, 0, 1, 1, 0, 2)], axis=0)
        at = jnp.concatenate([at, jnp.zeros((BLOCK - KDIM, BLOCK), bf16)], axis=0)
        a_ref[k] = mm(eye, at, nt=True).astype(bf16)


def twice(p):
    return jnp.concatenate([p, p], axis=1)


def spread(b):
    h, m, l = b[0:16], b[16:32], b[32:48]
    return jnp.concatenate([h, m, h, m, l, h], axis=0)


def twice_w(ww, s):
    return jnp.concatenate([ww[s, 0:BLOCK], ww[s, BLOCK:]], axis=1)


def weigh(qd, ww, s):
    r = lax.rsqrt(qd[s, :, BLOCK:])
    w = (qd[s, :, 0:BLOCK] * r) * (r * r)
    wh = w.astype(bf16)
    ww[s, 0:BLOCK] = wh
    ww[s, BLOCK:] = (w - wh.astype(f32)).astype(bf16)


def exchange(seg_in, cells_in, send_in, list_in, count, a_ref, b_ref, p_ref, self_ref, sure_ref, far_ref, mom_out,
             idx_out, inv_out, seg, cells, send_list, plist, ids, cnt, sib_seg, sib_ids, sib_cnt, sib_ghost,
             main, last, out_buf, in_buf, row, part, row2, table, qd, ww, l_sem, s_sem, r_sem, ss, sr,
             s1, r1, s2, r2):
    ix, iy = lax.axis_index("gx"), lax.axis_index("gy")
    sib = (ix, iy + 1 - 2 * lax.rem(iy, 2))
    loads = [
        pltpu.make_async_copy(src, dst, l_sem.at[n])
        for n, (src, dst) in enumerate(
            ((seg_in, seg), (send_in, send_list), (cells_in, cells), (list_in, plist), (list_in, ids))
        )
    ]
    for cp in loads:
        cp.start()
    barrier = pltpu.get_barrier_semaphore()

    def greet_y(o, _):
        pl.semaphore_signal(barrier, inc=1, device_id=(ix, lax.rem(iy + o, NY)), device_id_type=MESH)
        return 0

    def greet_x(o, _):
        pl.semaphore_signal(barrier, inc=1, device_id=(lax.rem(ix + o, NX), iy), device_id_type=MESH)
        return 0

    lax.fori_loop(1, NY, greet_y, 0)
    lax.fori_loop(1, NX, greet_x, 0)
    cnt[...] = jnp.full((1, BLOCK), count[0], i32)
    for cp in loads:
        cp.wait()
    for k in range(OWN):
        main[k] = seg[0:8, k * BLOCK : (k + 1) * BLOCK]
        last[k] = seg[8:9, k * BLOCK : (k + 1) * BLOCK]
    lanes = lax.broadcasted_iota(i32, (1, BLOCK), 1)
    for q in range(4):
        where = jnp.full((1, BLOCK), GHOST, i32)
        for j in range(GHOST):
            k = send_list[q, j]
            out_buf[q, 8 * j : 8 * j + 8, :] = main[k]
            out_buf[q, 8 * GHOST + j : 8 * GHOST + j + 1, :] = last[k]
            where = jnp.where(lanes == k, j, where)
        inv_out[q : q + 1, :] = where
    c = jnp.sum(seg[3:6, :] * seg[6:9, :], axis=0, keepdims=True)
    first = 2 * (ix * NY + iy)
    m0 = jnp.sum(jnp.where(cells[...] == first, c, 0.0))
    m1 = jnp.sum(jnp.where(cells[...] == first + 1, c, 0.0))
    mine = jnp.where(lanes == 2 * iy, m0, jnp.where(lanes == 2 * iy + 1, m1, 0.0))
    row[...] = mine
    part[NY - 1 : NY, :] = mine
    cx, cy = ix.astype(f32) + 0.5, iy.astype(f32) + 0.5
    sy = sib[1].astype(f32) + 0.5
    eye = eye128()

    def build_own(k, _):
        raw = jnp.concatenate([main[k], last[k]], axis=0)
        features(raw, cx, cy, eye, a_ref, b_ref, p_ref, k, True)
        weight = far_gain * jnp.sum(raw[3:6] * raw[6:9], axis=0, keepdims=True)
        far_ref[k] = jnp.concatenate([raw[0:2], raw[2:3] - 0.5, weight], axis=0)
        return 0

    lax.fori_loop(0, OWN, build_own, 0, unroll=4)
    pl.semaphore_wait(barrier, NY - 1 + NX - 1)
    copies = []
    for q, dev in enumerate(neighbours(ix, iy)):
        copies.append(
            pltpu.make_async_remote_copy(
                src_ref=out_buf.at[q], dst_ref=in_buf.at[q ^ 1], send_sem=s_sem.at[q],
                recv_sem=r_sem.at[q ^ 1], device_id=dev, device_id_type=MESH,
            )
        )
        copies[-1].start()

    def send_y(o, _):
        pltpu.make_async_remote_copy(
            src_ref=row, dst_ref=part.at[pl.ds(o - 1, 1)], send_sem=s1, recv_sem=r1,
            device_id=(ix, lax.rem(iy + o, NY)), device_id_type=MESH,
        ).start()
        return 0

    lax.fori_loop(1, NY, send_y, 0)
    shares = [
        pltpu.make_async_remote_copy(
            src_ref=src, dst_ref=dst, send_sem=ss.at[n], recv_sem=sr.at[n], device_id=sib, device_id_type=MESH
        )
        for n, (src, dst) in enumerate(((seg, sib_seg), (ids, sib_ids), (cnt, sib_cnt), (in_buf, sib_ghost)))
    ]
    for cp in shares[:3]:
        cp.start()

    def step(t, _):
        for s in range(GROUP):
            k = jnp.minimum(jnp.maximum((t - 2) * GROUP + s, 0), OWN - 1)
            self_ref[k] = mm(twice(p_ref[k]), ww[s])
            weigh(qd, ww, s)
            k = jnp.minimum(t * GROUP + s, OWN - 1)
            qd[s] = mm(a_ref[k][:, 0:KDIM], spread(b_ref[k]))
        return 0

    lax.fori_loop(0, OWN // GROUP + 2, step, 0)
    for cp in copies:
        cp.wait()
    shares[3].start()
    pltpu.make_async_copy(part.at[0 : NY - 1], part.at[0 : NY - 1], r1).wait()
    slab = jnp.sum(part[...], axis=0, keepdims=True)
    row2[...] = slab
    table[pl.ds(NX - 1, 1), :] = slab

    def send_x(o, _):
        pltpu.make_async_remote_copy(
            src_ref=row2, dst_ref=table.at[pl.ds(o - 1, 1)], send_sem=s2, recv_sem=r2,
            device_id=(lax.rem(ix + o, NX), iy), device_id_type=MESH,
        ).start()
        return 0

    lax.fori_loop(1, NX, send_x, 0)

    def ghosts_of(buf, cy, base):
        def build(j, _):
            for q in range(4):
                raw = jnp.concatenate(
                    [buf[q, pl.ds(pl.multiple_of(8 * j, 8), 8), :], buf[q, pl.ds(8 * GHOST + j, 1), :]], axis=0
                )
                features(raw, cx, cy, eye, a_ref, b_ref, p_ref, base + GHOST * q + j, False)
            return 0

        lax.fori_loop(0, GHOST, build, 0)

    ghosts_of(in_buf, cy, OWN)

    def sure_step(t, _):
        for s in range(GROUP):
            k = jnp.minimum(jnp.maximum((t - 2) * GROUP + s, 0), SURE - 1)
            i, j = plist[0, k], plist[1, k]
            sure_ref[k, 0] = mm(twice(p_ref[j]), twice_w(ww, s), nt=True)
            sure_ref[k, 1] = mm(twice(p_ref[i]), ww[s])
            weigh(qd, ww, s)
            k = jnp.minimum(t * GROUP + s, SURE - 1)
            i, j = plist[0, k], plist[1, k]
            qd[s] = mm(a_ref[i][:, 0:KDIM], spread(b_ref[j]))
        return 0

    lax.fori_loop(0, SURE // GROUP + 2, sure_step, 0)
    for cp in shares[:3]:
        cp.wait()

    def build_sib(k, _):
        raw = sib_seg[:, pl.ds(pl.multiple_of(k * BLOCK, BLOCK), BLOCK)]
        features(raw, cx, sy, eye, a_ref, b_ref, p_ref, SIB + k, True)
        return 0

    lax.fori_loop(0, OWN, build_sib, 0, unroll=4)
    idx_out[0:2, :] = ids[...]
    idx_out[2:4, :] = sib_ids[...] + SIB
    idx_out[4:5, :] = jnp.concatenate([cnt[...]] * (PAIRS // BLOCK), axis=1)
    idx_out[5:6, :] = jnp.concatenate([sib_cnt[...]] * (PAIRS // BLOCK), axis=1)
    shares[3].wait()
    ghosts_of(sib_ghost, sy, SIB + OWN)
    pltpu.make_async_copy(table.at[0 : NX - 1], table.at[0 : NX - 1], r2).wait()
    mom_out[...] = table[...]
    pltpu.make_async_copy(part.at[0 : NY - 1], part.at[0 : NY - 1], s1).wait()
    pltpu.make_async_copy(table.at[0 : NX - 1], table.at[0 : NX - 1], s2).wait()


def finish(acc, p):
    p = p.astype(f32)
    f = []
    for c in range(3):
        x = p[3 * c : 3 * c + 1] + p[3 * c + 1 : 3 * c + 2] + p[3 * c + 2 : 3 * c + 3]
        f.append(x * acc[9:10] - (acc[3 * c : 3 * c + 1] + acc[3 * c + 1 : 3 * c + 2] + acc[3 * c + 2 : 3 * c + 3]))
    return f


def pairs(idx, a_ref, b_ref, p_ref, self_ref, sure_ref, out, qd, ww, rr, acc_a, acc_b):
    own_rows, sib_rows = idx[4, 0] - SURE, idx[5, 0] - SURE
    half = (own_rows + sib_rows + 1) // 2
    n_own = jnp.minimum(own_rows, half)
    n_help = jnp.maximum(sib_rows - half, 0)
    total = n_own + n_help
    acc_a[0:OWN] = jnp.zeros((OWN, 16, BLOCK), f32)
    acc_b[0:OWN] = self_ref[...]
    acc_b[OWN:ALL] = jnp.zeros((ALL - OWN, 16, BLOCK), f32)

    @pl.when(n_help > 0)
    def _():
        acc_a[SIB : SIB + OWN] = jnp.zeros((OWN, 16, BLOCK), f32)
        acc_b[SIB : SIB + ALL] = jnp.zeros((ALL, 16, BLOCK), f32)

    def add_sure(k, _):
        acc_a[idx[0, k]] += sure_ref[k, 0]
        acc_b[idx[1, k]] += sure_ref[k, 1]
        return 0

    lax.fori_loop(0, SURE, add_sure, 0, unroll=8)

    def pick(r):
        r = jnp.maximum(jnp.minimum(r, total - 1), 0)
        own = r < n_own
        at = r + jnp.where(own, SURE, SURE + half - n_own)
        which = jnp.where(own, 0, 2)
        return idx[which, at], idx[which + 1, at]

    def step(t, _):
        for s in range(GROUP):
            r = (t - 3) * GROUP + s
            i, j = pick(r)
            live = jnp.logical_and(r >= 0, r < total)
            acc_a[jnp.where(live, i, TRASH)] += rr[s, 0]
            acc_b[jnp.where(live, j, TRASH)] += rr[s, 1]
            i, j = pick((t - 2) * GROUP + s)
            rr[s, 0] = mm(twice(p_ref[j]), twice_w(ww, s), nt=True)
            rr[s, 1] = mm(twice(p_ref[i]), ww[s])
            weigh(qd, ww, s)
            i, j = pick(t * GROUP + s)
            qd[s] = mm(a_ref[i][:, 0:KDIM], spread(b_ref[j]))
        return 0

    @pl.when(total > 0)
    def _():
        lax.fori_loop(0, (total + GROUP - 1) // GROUP + 3, step, 0)

    zero = jnp.zeros((1, BLOCK), f32)

    def finish_own(k, _):
        out[k] = jnp.concatenate(finish(acc_a[k] + acc_b[k], p_ref[k]) + [zero], axis=0)
        return 0

    def finish_other(k, _):
        out[k] = jnp.concatenate(finish(acc_b[k], p_ref[k]) + [zero], axis=0)
        return 0

    lax.fori_loop(0, OWN, finish_own, 0, unroll=4)
    lax.fori_loop(OWN, ALL, finish_other, 0, unroll=4)

    @pl.when(n_help > 0)
    def _():
        lax.fori_loop(SIB, SIB + OWN, finish_own, 0, unroll=4)
        lax.fori_loop(SIB + OWN, SIB + ALL, finish_other, 0, unroll=4)

    @pl.when(n_help == 0)
    def _():
        out[SIB:] = jnp.zeros((ALL, 4, BLOCK), f32)


def finale(inv, far_ref, mom, force, out, sib_in, gsum, back_in, mb, ss, sr, s_sem, r_sem):
    ix, iy = lax.axis_index("gx"), lax.axis_index("gy")
    sib = (ix, iy + 1 - 2 * lax.rem(iy, 2))
    barrier = pltpu.get_barrier_semaphore()
    near = neighbours(ix, iy)
    for dev in near:
        pl.semaphore_signal(barrier, inc=1, device_id=dev, device_id_type=MESH)
    for q in range(4):
        back_in[q, GHOST] = jnp.zeros((4, BLOCK), f32)
    pl.semaphore_wait(barrier, 4)
    share = pltpu.make_async_remote_copy(
        src_ref=force.at[SIB : SIB + ALL], dst_ref=sib_in, send_sem=ss, recv_sem=sr, device_id=sib,
        device_id_type=MESH,
    )
    share.start()
    wide = jnp.concatenate([mom[...], jnp.zeros((BLOCK - NX, BLOCK), f32)], axis=0).T
    for s in range(NX):
        mb[s] = jnp.broadcast_to(wide[0 : 2 * NY, s : s + 1], (2 * NY, BLOCK))
    centre_x = [lax.rem(ix + (2 * NX - 1 - s), NX).astype(f32) + 0.5 for s in range(NX)]
    sub = lax.broadcasted_iota(i32, (8, BLOCK), 0).astype(f32)
    share.wait()
    gsum[...] = force[OWN:ALL] + sib_in[OWN:ALL]
    copies = []
    for q, dev in enumerate(near):
        copies.append(
            pltpu.make_async_remote_copy(
                src_ref=gsum.at[GHOST * q : GHOST * q + GHOST], dst_ref=back_in.at[q ^ 1, 0:GHOST],
                send_sem=s_sem.at[q], recv_sem=r_sem.at[q ^ 1], device_id=dev, device_id_type=MESH,
            )
        )
        copies[-1].start()

    def far(k, _):
        blk = far_ref[k]
        x, y, z = jnp.broadcast_to(blk[0:1], (8, BLOCK)), jnp.broadcast_to(blk[1:2], (8, BLOCK)), blk[2:3]
        base = z * z + far_core_sq
        dx = [x - cx for cx in centre_x]
        dx2 = [d * d for d in dx]
        hx = [None] * NX
        fy = total = None
        for g in range(2 * NY // 8):
            dy = y - (0.5 * sub + (4.0 * g + 0.25))
            by = dy * dy + base
            gy = None
            for s in range(NX):
                r = lax.rsqrt(by + dx2[s])
                w = (mb[s, 8 * g : 8 * g + 8, :] * r) * (r * r)
                hx[s] = w if g == 0 else hx[s] + w
                gy = w if s == 0 else gy + w
            total = gy if g == 0 else total + gy
            fy = dy * gy if g == 0 else fy + dy * gy
        fx = dx[0] * hx[0]
        for s in range(1, NX):
            fx = fx + dx[s] * hx[s]
        add = lambda t: jnp.sum(t, axis=0, keepdims=True)
        f = jnp.concatenate([add(fx), add(fy), z * add(total)], axis=0)
        where = pl.ds(pl.multiple_of(k * BLOCK, BLOCK), BLOCK)
        out[:, where] = blk[3:4] * f + (force[k] + sib_in[k])[0:3]
        return 0

    lax.fori_loop(0, OWN, far, 0)
    for cp in copies:
        cp.wait()

    def combine(k, _):
        f = back_in[0, inv[0, k]]
        for q in range(1, 4):
            f = f + back_in[q, inv[q, k]]
        where = pl.ds(pl.multiple_of(k * BLOCK, BLOCK), BLOCK)
        out[:, where] = out[:, where] + f[0:3]
        return 0

    lax.fori_loop(0, OWN, combine, 0, unroll=4)


VM, SM = pl.BlockSpec(memory_space=pltpu.VMEM), pl.BlockSpec(memory_space=pltpu.SMEM)
HB = pl.BlockSpec(memory_space=pltpu.HBM)
SDS = jax.ShapeDtypeStruct
DMA = pltpu.SemaphoreType.DMA


def body(segments, pair_list, pair_count, send_list, cell_ids):
    segs = segments.shape[1]
    a, b, p, own_sums, sure, far, mom, idx, inv = pl.pallas_call(
        exchange,
        name="exchange",
        out_shape=(
            SDS((SIB + OWN, BLOCK, BLOCK), bf16),
            SDS((2 * ALL, 48, 2 * BLOCK), bf16),
            SDS((2 * ALL, 16, BLOCK), bf16),
            SDS((OWN, 16, BLOCK), f32),
            SDS((SURE, 2, 16, BLOCK), f32),
            SDS((OWN, 4, BLOCK), f32),
            SDS((NX, BLOCK), f32),
            SDS((6, PAIRS), i32),
            SDS((4, BLOCK), i32),
        ),
        in_specs=[HB, HB, HB, HB, SM],
        out_specs=(VM,) * 9,
        scratch_shapes=[
            pltpu.VMEM((9, segs), f32),
            pltpu.VMEM((1, segs), i32),
            pltpu.SMEM((4, GHOST), i32),
            pltpu.SMEM((2, PAIRS), i32),
            pltpu.VMEM((2, PAIRS), i32),
            pltpu.VMEM((1, BLOCK), i32),
            pltpu.VMEM((9, segs), f32),
            pltpu.VMEM((2, PAIRS), i32),
            pltpu.VMEM((1, BLOCK), i32),
            pltpu.VMEM((4, ROWS, BLOCK), f32),
            pltpu.VMEM((OWN, 8, BLOCK), f32),
            pltpu.VMEM((OWN, 1, BLOCK), f32),
            pltpu.VMEM((4, ROWS, BLOCK), f32),
            pltpu.VMEM((4, ROWS, BLOCK), f32),
            pltpu.VMEM((1, BLOCK), f32),
            pltpu.VMEM((NY, BLOCK), f32),
            pltpu.VMEM((1, BLOCK), f32),
            pltpu.VMEM((NX, BLOCK), f32),
            pltpu.VMEM((GROUP, BLOCK, 2 * BLOCK), f32),
            pltpu.VMEM((GROUP, 2 * BLOCK, BLOCK), bf16),
            DMA((5,)), DMA((4,)), DMA((4,)), DMA((4,)), DMA((4,)), DMA, DMA, DMA, DMA,
        ],
        compiler_params=pltpu.CompilerParams(
            collective_id=0, has_side_effects=True, vmem_limit_bytes=24 * 2**20
        ),
    )(segments, cell_ids.reshape(1, -1), send_list, pair_list.T, pair_count)
    force = pl.pallas_call(
        pairs,
        name="pairs",
        out_shape=SDS((2 * ALL, 4, BLOCK), f32),
        in_specs=[SM] + [VM] * 5,
        out_specs=VM,
        scratch_shapes=[
            pltpu.VMEM((GROUP, BLOCK, 2 * BLOCK), f32),
            pltpu.VMEM((GROUP, 2 * BLOCK, BLOCK), bf16),
            pltpu.VMEM((GROUP, 2, 16, BLOCK), f32),
            pltpu.VMEM((2 * ALL + 1, 16, BLOCK), f32),
            pltpu.VMEM((2 * ALL + 1, 16, BLOCK), f32),
        ],
        compiler_params=pltpu.CompilerParams(vmem_limit_bytes=24 * 2**20),
    )(idx, a, b, p, own_sums, sure)
    return pl.pallas_call(
        finale,
        name="finale",
        out_shape=SDS((3, segs), f32),
        in_specs=[SM, VM, VM, VM],
        out_specs=VM,
        scratch_shapes=[
            pltpu.VMEM((ALL, 4, BLOCK), f32),
            pltpu.VMEM((4 * GHOST, 4, BLOCK), f32),
            pltpu.VMEM((4, GHOST + 1, 4, BLOCK), f32),
            pltpu.VMEM((NX, 2 * NY, BLOCK), f32),
            DMA, DMA, DMA((4,)), DMA((4,)),
        ],
        compiler_params=pltpu.CompilerParams(
            collective_id=1, has_side_effects=True, vmem_limit_bytes=16 * 2**20
        ),
    )(inv, far, mom, force)


def solution(mesh):
    in_specs = (
        P(None, ("gx", "gy")),
        P(("gx", "gy"), None),
        P(("gx", "gy")),
        P(("gx", "gy"), None),
        P(("gx", "gy")),
    )
    out_specs = P(None, ("gx", "gy"))
    return jax.shard_map(body, mesh=mesh, in_specs=in_specs, out_specs=out_specs, check_vma=False)
```

time: 67.7 us -> 58.9 us (0.87)
  the two profiles are of different devices: /device:TPU:121 before, /device:TPU:1 now
where the time goes in v3:
time: 58.9 us; the launch traced here: 58.6 us
  Pallas kernels  54.1 us (92%)
  local copies, waits for them, and re-layouts  3.82 us (6%)
  between operations  0.69 us (1%)
    pallas_call x1, Pallas kernels, body(): pl.pallas_call(exchange, name='exchange', out_shape=(SDS((SIB + OWN, BLOC...  28 us
    pallas_call x1, Pallas kernels, body(): pl.pallas_call(finale, name='finale', out_shape=SDS((3, segs), f32), in_s...  20.2 us
    pallas_call x1, Pallas kernels, body(): pl.pallas_call(pairs, name='pairs', out_shape=SDS((2 * ALL, 4, BLOCK), f3...  5.97 us
    unnamed x9, local copies, waits for them, and re-layouts  3.82 us

profile of v3, /device:TPU:1, one launch (start us, length us, event | category | flops | bytes accessed | tf_op | source)
XLA Modules:
  0.0 58.6 jit_solution(1690003034053919143)
XLA Ops:
  0.7 0.0 copy-start
  0.7 1.0 %copy-done = f32[9,8192]{1,0:T(8,128)S(1)} copy-done((f32[9,8192]{1,0:T(8,128)S(1)}, f32[9,8192]{1,0:T(8,128)}, u32[]{:S(2)}) %copy-start) | copy-done | bytes 294936
  1.7 0.0 copy-start.1
  1.7 0.8 %copy-done.1 = s32[8192]{0:T(1024)S(1)} copy-done((s32[8192]{0:T(1024)S(1)}, s32[8192]{0:T(1024)}, u32[]{:S(2)}) %copy-start.1) | copy-done | bytes 32792
  2.5 0.0 copy-start.2
  2.5 0.7 %copy-done.2 = s32[512,2]{0,1:T(2,128)S(1)} copy-done((s32[512,2]{0,1:T(2,128)S(1)}, s32[512,2]{0,1:T(2,128)}, u32[]{:S(2)}) %copy-start.2) | copy-done | bytes 4120
  3.1 0.0 copy-start.3
  3.1 0.7 %copy-done.3 = s32[4,16]{1,0:T(4,128)S(1)} copy-done((s32[4,16]{1,0:T(4,128)S(1)}, s32[4,16]{1,0:T(4,128)}, u32[]{:S(2)}) %copy-start.3) | copy-done | bytes 280
  3.8 28.0 %exchange.1 = (bf16[192,128,128]{2,1,0:T(8,128)(2,1)S(1)}, bf16[256,48,256]{2,1,0:T(8,128)(2,1)S(1)}, bf16[256,16,128]{2,1,0:T(8,128)(2,1)S(1)}, f32[64,16,128]{...) custom-call(f32[9,8192]{1,0:T(8,128)S(1)} %copy-done, ...), custom_call_target="tpu_custom_call" | custom-call | tf_op jit(solution)/shard_map/exchange/pallas_call | solution.py:432
  31.8 6.0 %pairs.1.force = f32[256,4,128]{2,1,0:T(4,128)S(1)} custom-call(s32[6,512]{1,0:T(8,128)S(1)} %get-tuple-element.17.idx, bf16[192,128,128]{2,1,0:T(8,128)(2,1)S(1)} %get-tuple-element.18.a_ref, bf16[256,48,256]{2,1,0:T(8,128)(2,1)S(1)} %get-tuple-element.19.b_ref, bf16[256,16,128]{2,1,0:T(8,128)(2,1)S(1)} %get-tuple-element.20.p_ref, ...), custom_call_target="tpu_custom_call" | custom-call | tf_op jit(solution)/shard_map/pairs/pallas_call | solution.py:475
  37.8 20.2 %finale.1 = f32[3,8192]{1,0:T(4,128)S(1)} custom-call(s32[4,128]{1,0:T(4,128)S(1)} %get-tuple-element.14.inv, f32[64,4,128]{2,1,0:T(4,128)S(1)} %get-tuple-element.15.far_ref, f32[8,128]{1,0:T(8,128)S(1)} %get-tuple-element.16.mom, f32[256,4,128]{2,1,0:T(4,128)S(1)} %pairs.1.force), custom_call_target="tpu_custom_call" | custom-call | tf_op jit(solution)/shard_map/finale/pallas_call | solution.py:490
  58.0 0.7 %copy.8 = f32[3,8192]{1,0:T(4,128)} copy(f32[3,8192]{1,0:T(4,128)S(1)} %finale.1) | data formatting | bytes 196608
Async XLA Ops:
  0.7 1.0 %copy-start = (f32[9,8192]{1,0:T(8,128)S(1)}, f32[9,8192]{1,0:T(8,128)}, u32[]{:S(2)}) copy-start(f32[9,8192]{1,0:T(8,128)} %seg_in.1) | copy-start | bytes 884740
  1.7 0.8 %copy-start.1 = (s32[8192]{0:T(1024)S(1)}, s32[8192]{0:T(1024)}, u32[]{:S(2)}) copy-start(s32[8192]{0:T(1024)} %param.9) | copy-start | bytes 98308
  2.5 0.7 %copy-start.2 = (s32[512,2]{0,1:T(2,128)S(1)}, s32[512,2]{0,1:T(2,128)}, u32[]{:S(2)}) copy-start(s32[512,2]{0,1:T(2,128)} %param.6) | copy-start | bytes 12292
  3.1 0.7 %copy-start.3 = (s32[4,16]{1,0:T(4,128)S(1)}, s32[4,16]{1,0:T(4,128)}, u32[]{:S(2)}) copy-start(s32[4,16]{1,0:T(4,128)} %send_in.1) | copy-start | bytes 772

commit v4 on v3

--- a/solution.py
+++ b/solution.py
@@ -18,7 +18,7 @@
 SURE = 64
 PAIRS = 512
 NX, NY = 8, 32
-GROUP = 8
+GROUP = 16
 KDIM = 96
 ROWS = 9 * GHOST
 
@@ -42,9 +42,7 @@
 
 def rows16(parts):
     missing = 16 - sum(p.shape[0] for p in parts)
-    if missing:
-        parts = parts + [jnp.zeros((missing, BLOCK), f32)]
-    return jnp.concatenate(parts, axis=0)
+    return jnp.concatenate(parts + [jnp.zeros((missing, BLOCK), f32)], axis=0)
 
 
 def eye128():
@@ -61,26 +59,25 @@
     )
 
 
-def features(raw, cx, cy, eye, a_ref, b_ref, p_ref, k, with_a):
-    k = jnp.int32(k) if isinstance(k, int) else k
-    x, y, z = raw[0:1] - cx, raw[1:2] - cy, raw[2:3] - 0.5
+def features(raw, centre, eye, a_ref, b_ref, p_ref, k, with_a):
+    pos = raw[0:3] - centre
     l, b = raw[3:6], raw[6:9]
-    u = [b[0:1] * l, b[1:2] * l, b[2:3] * l]
-    norm = x * x + y * y + z * z
+    u = jnp.concatenate([b[0:1] * l, b[1:2] * l, b[2:3] * l], axis=0)
+    norm = jnp.sum(pos * pos, axis=0, keepdims=True)
     one = jnp.ones((1, BLOCK), f32)
-    bq = split3(rows16(u))
-    bd = split3(rows16([jnp.zeros((9, BLOCK), f32), x, y, z, norm, one]))
-    b_ref[k, :, 0:BLOCK] = jnp.concatenate(bq, axis=0)
-    b_ref[k, :, BLOCK:] = jnp.concatenate(bd, axis=0)
-    pos = [t.astype(f32) for t in split3(x) + split3(y) + split3(z)]
-    p_ref[k] = rows16(pos + [one]).astype(bf16)
+    zero9 = jnp.zeros((9, BLOCK), f32)
+    b_ref[k, :, 0:BLOCK] = jnp.concatenate(split3(rows16([u])), axis=0)
+    b_ref[k, :, BLOCK:] = jnp.concatenate(split3(rows16([zero9, pos, norm, one])), axis=0)
+    p_ref[k] = rows16([t.astype(f32) for t in split3(pos)] + [one]).astype(bf16)
     if with_a:
-        fa = split3(
-            rows16([strength * t for t in u] + [-2.0 * x, -2.0 * y, -2.0 * z, one, norm + core_sq])
-        )
-        at = jnp.concatenate([fa[o] for o in (0, 0, 1, 1, 0, 2)], axis=0)
-        at = jnp.concatenate([at, jnp.zeros((BLOCK - KDIM, BLOCK), bf16)], axis=0)
+        h, m, l = split3(rows16([strength * u, -2.0 * pos, one, norm + core_sq]))
+        at = jnp.concatenate([h, h, m, m, h, l, jnp.zeros((BLOCK - KDIM, BLOCK), bf16)], axis=0)
         a_ref[k] = mm(eye, at, nt=True).astype(bf16)
+
+
+def centre_of(ix, iy):
+    r = lax.broadcasted_iota(i32, (3, BLOCK), 0)
+    return jnp.where(r == 0, ix.astype(f32), jnp.where(r == 1, iy.astype(f32), 0.0)) + 0.5
 
 
 def twice(p):
@@ -90,22 +87,36 @@
 def spread(b):
     h, m, l = b[0:16], b[16:32], b[32:48]
     return jnp.concatenate([h, m, h, m, l, h], axis=0)
-
-
-def twice_w(ww, s):
-    return jnp.concatenate([ww[s, 0:BLOCK], ww[s, BLOCK:]], axis=1)
 
 
 def weigh(qd, ww, s):
     r = lax.rsqrt(qd[s, :, BLOCK:])
     w = (qd[s, :, 0:BLOCK] * r) * (r * r)
     wh = w.astype(bf16)
-    ww[s, 0:BLOCK] = wh
-    ww[s, BLOCK:] = (w - wh.astype(f32)).astype(bf16)
+    half = slice(0, BLOCK) if s % 2 == 0 else slice(BLOCK, 2 * BLOCK)
+    ww[s // 2, 0:BLOCK, half] = wh
+    ww[s // 2, BLOCK:, half] = (w - wh.astype(f32)).astype(bf16)
+
+
+def sums_over(w, p0, p1):
+    f = mm(jnp.concatenate([twice(p0), twice(p1)], axis=0), w)
+    return f[0:16, 0:BLOCK], f[16:32, BLOCK:]
+
+
+def second_sums(ww, s, p0, p1):
+    return sums_over(ww[s], p0, p1)
+
+
+def first_sums(ww, s, p0, p1):
+    w = ww[s]
+    turned = [
+        jnp.concatenate([w[r : r + BLOCK, 0:BLOCK].T, w[r : r + BLOCK, BLOCK:].T], axis=1) for r in (0, BLOCK)
+    ]
+    return sums_over(jnp.concatenate(turned, axis=0), p0, p1)
 
 
 def exchange(seg_in, cells_in, send_in, list_in, count, a_ref, b_ref, p_ref, self_ref, sure_ref, far_ref, mom_out,
-             idx_out, inv_out, seg, cells, send_list, plist, ids, cnt, sib_seg, sib_ids, sib_cnt, sib_ghost,
+             idx_out, cnt_out, inv_out, seg, cells, send_list, plist, ids, cnt, sib_seg, sib_ids, sib_cnt, sib_ghost,
              main, last, out_buf, in_buf, row, part, row2, table, qd, ww, l_sem, s_sem, r_sem, ss, sr,
              s1, r1, s2, r2):
     ix, iy = lax.axis_index("gx"), lax.axis_index("gy")
@@ -152,13 +163,12 @@
     mine = jnp.where(lanes == 2 * iy, m0, jnp.where(lanes == 2 * iy + 1, m1, 0.0))
     row[...] = mine
     part[NY - 1 : NY, :] = mine
-    cx, cy = ix.astype(f32) + 0.5, iy.astype(f32) + 0.5
-    sy = sib[1].astype(f32) + 0.5
+    centre, sib_centre = centre_of(ix, iy), centre_of(ix, sib[1])
     eye = eye128()
 
     def build_own(k, _):
         raw = jnp.concatenate([main[k], last[k]], axis=0)
-        features(raw, cx, cy, eye, a_ref, b_ref, p_ref, k, True)
+        features(raw, centre, eye, a_ref, b_ref, p_ref, k, True)
         weight = far_gain * jnp.sum(raw[3:6] * raw[6:9], axis=0, keepdims=True)
         far_ref[k] = jnp.concatenate([raw[0:2], raw[2:3] - 0.5, weight], axis=0)
         return 0
@@ -193,15 +203,26 @@
         cp.start()
 
     def step(t, _):
-        for s in range(GROUP):
-            k = jnp.minimum(jnp.maximum((t - 2) * GROUP + s, 0), OWN - 1)
-            self_ref[k] = mm(twice(p_ref[k]), ww[s])
+        for s in range(0, GROUP, 2):
+            k = jnp.minimum(jnp.maximum((t - 2) * GROUP + s, 0), OWN - 2)
+            self_ref[k], self_ref[k + 1] = second_sums(ww, s // 2, p_ref[k], p_ref[k + 1])
             weigh(qd, ww, s)
-            k = jnp.minimum(t * GROUP + s, OWN - 1)
+            weigh(qd, ww, s + 1)
+            k = jnp.minimum(t * GROUP + s, OWN - 2)
             qd[s] = mm(a_ref[k][:, 0:KDIM], spread(b_ref[k]))
+            qd[s + 1] = mm(a_ref[k + 1][:, 0:KDIM], spread(b_ref[k + 1]))
         return 0
 
     lax.fori_loop(0, OWN // GROUP + 2, step, 0)
+    for cp in shares[:3]:
+        cp.wait()
+
+    def build_sib(k, _):
+        raw = sib_seg[:, pl.ds(pl.multiple_of(k * BLOCK, BLOCK), BLOCK)]
+        features(raw, sib_centre, eye, a_ref, b_ref, p_ref, SIB + k, True)
+        return 0
+
+    lax.fori_loop(0, OWN, build_sib, 0, unroll=4)
     for cp in copies:
         cp.wait()
     shares[3].start()
@@ -219,47 +240,39 @@
 
     lax.fori_loop(1, NX, send_x, 0)
 
-    def ghosts_of(buf, cy, base):
+    def ghosts_of(buf, cen, base):
         def build(j, _):
             for q in range(4):
                 raw = jnp.concatenate(
                     [buf[q, pl.ds(pl.multiple_of(8 * j, 8), 8), :], buf[q, pl.ds(8 * GHOST + j, 1), :]], axis=0
                 )
-                features(raw, cx, cy, eye, a_ref, b_ref, p_ref, base + GHOST * q + j, False)
+                features(raw, cen, eye, a_ref, b_ref, p_ref, base + GHOST * q + j, False)
             return 0
 
         lax.fori_loop(0, GHOST, build, 0)
 
-    ghosts_of(in_buf, cy, OWN)
+    ghosts_of(in_buf, centre, OWN)
 
     def sure_step(t, _):
-        for s in range(GROUP):
-            k = jnp.minimum(jnp.maximum((t - 2) * GROUP + s, 0), SURE - 1)
-            i, j = plist[0, k], plist[1, k]
-            sure_ref[k, 0] = mm(twice(p_ref[j]), twice_w(ww, s), nt=True)
-            sure_ref[k, 1] = mm(twice(p_ref[i]), ww[s])
+        for s in range(0, GROUP, 2):
+            k = jnp.minimum(jnp.maximum((t - 2) * GROUP + s, 0), SURE - 2)
+            sure_ref[k, 0], sure_ref[k + 1, 0] = first_sums(ww, s // 2, p_ref[plist[1, k]], p_ref[plist[1, k + 1]])
+            sure_ref[k, 1], sure_ref[k + 1, 1] = second_sums(ww, s // 2, p_ref[plist[0, k]], p_ref[plist[0, k + 1]])
             weigh(qd, ww, s)
-            k = jnp.minimum(t * GROUP + s, SURE - 1)
-            i, j = plist[0, k], plist[1, k]
-            qd[s] = mm(a_ref[i][:, 0:KDIM], spread(b_ref[j]))
+            weigh(qd, ww, s + 1)
+            k = jnp.minimum(t * GROUP + s, SURE - 2)
+            for d in range(2):
+                qd[s + d] = mm(a_ref[plist[0, k + d]][:, 0:KDIM], spread(b_ref[plist[1, k + d]]))
         return 0
 
     lax.fori_loop(0, SURE // GROUP + 2, sure_step, 0)
-    for cp in shares[:3]:
-        cp.wait()
-
-    def build_sib(k, _):
-        raw = sib_seg[:, pl.ds(pl.multiple_of(k * BLOCK, BLOCK), BLOCK)]
-        features(raw, cx, sy, eye, a_ref, b_ref, p_ref, SIB + k, True)
-        return 0
-
-    lax.fori_loop(0, OWN, build_sib, 0, unroll=4)
     idx_out[0:2, :] = ids[...]
     idx_out[2:4, :] = sib_ids[...] + SIB
-    idx_out[4:5, :] = jnp.concatenate([cnt[...]] * (PAIRS // BLOCK), axis=1)
-    idx_out[5:6, :] = jnp.concatenate([sib_cnt[...]] * (PAIRS // BLOCK), axis=1)
+    idx_out[4:8, :] = jnp.zeros((4, PAIRS), i32)
+    cnt_out[0:1, :] = cnt[...]
+    cnt_out[1:2, :] = sib_cnt[...]
     shares[3].wait()
-    ghosts_of(sib_ghost, sy, SIB + OWN)
+    ghosts_of(sib_ghost, sib_centre, SIB + OWN)
     pltpu.make_async_copy(table.at[0 : NX - 1], table.at[0 : NX - 1], r2).wait()
     mom_out[...] = table[...]
     pltpu.make_async_copy(part.at[0 : NY - 1], part.at[0 : NY - 1], s1).wait()
@@ -268,19 +281,31 @@
 
 def finish(acc, p):
     p = p.astype(f32)
-    f = []
-    for c in range(3):
-        x = p[3 * c : 3 * c + 1] + p[3 * c + 1 : 3 * c + 2] + p[3 * c + 2 : 3 * c + 3]
-        f.append(x * acc[9:10] - (acc[3 * c : 3 * c + 1] + acc[3 * c + 1 : 3 * c + 2] + acc[3 * c + 2 : 3 * c + 3]))
-    return f
-
-
-def pairs(idx, a_ref, b_ref, p_ref, self_ref, sure_ref, out, qd, ww, rr, acc_a, acc_b):
-    own_rows, sib_rows = idx[4, 0] - SURE, idx[5, 0] - SURE
+    f = (p[0:3] + p[3:6] + p[6:9]) * acc[9:10] - (acc[0:3] + acc[3:6] + acc[6:9])
+    return jnp.concatenate([f, jnp.zeros((1, BLOCK), f32)], axis=0)
+
+
+def pairs(counts, lists, a_ref, b_ref, p_ref, self_ref, sure_ref, out, merged, rows, qd, ww, rr, acc_a, acc_b, sem):
+    own_rows, sib_rows = counts[0, 0] - SURE, counts[1, 0] - SURE
     half = (own_rows + sib_rows + 1) // 2
     n_own = jnp.minimum(own_rows, half)
     n_help = jnp.maximum(sib_rows - half, 0)
     total = n_own + n_help
+    r = lax.broadcasted_iota(i32, (1, PAIRS), 1) - 2 * GROUP
+    skip = SURE - 2 * GROUP
+    own_list = pltpu.roll(lists[...], PAIRS - skip, 1)
+    sib_list = pltpu.roll(lists[...], PAIRS - (skip + half - n_own), 1)
+    live = jnp.logical_and(r >= 0, r < total)
+    i = jnp.where(r < n_own, own_list[0:1], sib_list[2:3])
+    j = jnp.where(r < n_own, own_list[1:2], sib_list[3:4])
+    merged[0:1, :] = jnp.where(live, i, 0)
+    merged[1:2, :] = jnp.where(live, j, 0)
+    merged[2:3, :] = jnp.where(live, i, TRASH)
+    merged[3:4, :] = jnp.where(live, j, TRASH)
+    merged[4:6, :] = lists[0:2, :]
+    merged[6:8, :] = jnp.zeros((2, PAIRS), i32)
+    fetch = pltpu.make_async_copy(merged, rows, sem)
+    fetch.start()
     acc_a[0:OWN] = jnp.zeros((OWN, 16, BLOCK), f32)
     acc_b[0:OWN] = self_ref[...]
     acc_b[OWN:ALL] = jnp.zeros((ALL - OWN, 16, BLOCK), f32)
@@ -290,47 +315,41 @@
         acc_a[SIB : SIB + OWN] = jnp.zeros((OWN, 16, BLOCK), f32)
         acc_b[SIB : SIB + ALL] = jnp.zeros((ALL, 16, BLOCK), f32)
 
+    fetch.wait()
+
     def add_sure(k, _):
-        acc_a[idx[0, k]] += sure_ref[k, 0]
-        acc_b[idx[1, k]] += sure_ref[k, 1]
+        acc_a[rows[4, k]] += sure_ref[k, 0]
+        acc_b[rows[5, k]] += sure_ref[k, 1]
         return 0
 
     lax.fori_loop(0, SURE, add_sure, 0, unroll=8)
 
-    def pick(r):
-        r = jnp.maximum(jnp.minimum(r, total - 1), 0)
-        own = r < n_own
-        at = r + jnp.where(own, SURE, SURE + half - n_own)
-        which = jnp.where(own, 0, 2)
-        return idx[which, at], idx[which + 1, at]
-
     def step(t, _):
+        for s in range(0, GROUP, 2):
+            c = t * GROUP + s
+            rr[s, 0], rr[s + 1, 0] = first_sums(ww, s // 2, p_ref[rows[1, c]], p_ref[rows[1, c + 1]])
+            rr[s, 1], rr[s + 1, 1] = second_sums(ww, s // 2, p_ref[rows[0, c]], p_ref[rows[0, c + 1]])
+            weigh(qd, ww, s)
+            weigh(qd, ww, s + 1)
+            c = c + 2 * GROUP
+            for d in range(2):
+                qd[s + d] = mm(a_ref[rows[0, c + d]][:, 0:KDIM], spread(b_ref[rows[1, c + d]]))
         for s in range(GROUP):
-            r = (t - 3) * GROUP + s
-            i, j = pick(r)
-            live = jnp.logical_and(r >= 0, r < total)
-            acc_a[jnp.where(live, i, TRASH)] += rr[s, 0]
-            acc_b[jnp.where(live, j, TRASH)] += rr[s, 1]
-            i, j = pick((t - 2) * GROUP + s)
-            rr[s, 0] = mm(twice(p_ref[j]), twice_w(ww, s), nt=True)
-            rr[s, 1] = mm(twice(p_ref[i]), ww[s])
-            weigh(qd, ww, s)
-            i, j = pick(t * GROUP + s)
-            qd[s] = mm(a_ref[i][:, 0:KDIM], spread(b_ref[j]))
+            c = t * GROUP + s
+            acc_a[rows[2, c]] += rr[s, 0]
+            acc_b[rows[3, c]] += rr[s, 1]
         return 0
 
     @pl.when(total > 0)
     def _():
-        lax.fori_loop(0, (total + GROUP - 1) // GROUP + 3, step, 0)
-
-    zero = jnp.zeros((1, BLOCK), f32)
+        lax.fori_loop(0, (total + GROUP - 1) // GROUP + 2, step, 0)
 
     def finish_own(k, _):
-        out[k] = jnp.concatenate(finish(acc_a[k] + acc_b[k], p_ref[k]) + [zero], axis=0)
+        out[k] = finish(acc_a[k] + acc_b[k], p_ref[k])
         return 0
 
     def finish_other(k, _):
-        out[k] = jnp.concatenate(finish(acc_b[k], p_ref[k]) + [zero], axis=0)
+        out[k] = finish(acc_b[k], p_ref[k])
         return 0
 
     lax.fori_loop(0, OWN, finish_own, 0, unroll=4)
@@ -366,18 +385,6 @@
         mb[s] = jnp.broadcast_to(wide[0 : 2 * NY, s : s + 1], (2 * NY, BLOCK))
     centre_x = [lax.rem(ix + (2 * NX - 1 - s), NX).astype(f32) + 0.5 for s in range(NX)]
     sub = lax.broadcasted_iota(i32, (8, BLOCK), 0).astype(f32)
-    share.wait()
-    gsum[...] = force[OWN:ALL] + sib_in[OWN:ALL]
-    copies = []
-    for q, dev in enumerate(near):
-        copies.append(
-            pltpu.make_async_remote_copy(
-                src_ref=gsum.at[GHOST * q : GHOST * q + GHOST], dst_ref=back_in.at[q ^ 1, 0:GHOST],
-                send_sem=s_sem.at[q], recv_sem=r_sem.at[q ^ 1], device_id=dev, device_id_type=MESH,
-            )
-        )
-        copies[-1].start()
-
     def far(k, _):
         blk = far_ref[k]
         x, y, z = jnp.broadcast_to(blk[0:1], (8, BLOCK)), jnp.broadcast_to(blk[1:2], (8, BLOCK)), blk[2:3]
@@ -403,16 +410,29 @@
         add = lambda t: jnp.sum(t, axis=0, keepdims=True)
         f = jnp.concatenate([add(fx), add(fy), z * add(total)], axis=0)
         where = pl.ds(pl.multiple_of(k * BLOCK, BLOCK), BLOCK)
-        out[:, where] = blk[3:4] * f + (force[k] + sib_in[k])[0:3]
-        return 0
-
-    lax.fori_loop(0, OWN, far, 0)
+        out[:, where] = blk[3:4] * f
+        return 0
+
+    lax.fori_loop(0, OWN // 4, far, 0)
+    share.wait()
+    gsum[...] = force[OWN:ALL] + sib_in[OWN:ALL]
+    copies = []
+    for q, dev in enumerate(near):
+        copies.append(
+            pltpu.make_async_remote_copy(
+                src_ref=gsum.at[GHOST * q : GHOST * q + GHOST], dst_ref=back_in.at[q ^ 1, 0:GHOST],
+                send_sem=s_sem.at[q], recv_sem=r_sem.at[q ^ 1], device_id=dev, device_id_type=MESH,
+            )
+        )
+        copies[-1].start()
+
+    lax.fori_loop(OWN // 4, OWN, far, 0)
     for cp in copies:
         cp.wait()
 
     def combine(k, _):
-        f = back_in[0, inv[0, k]]
-        for q in range(1, 4):
+        f = force[k] + sib_in[k]
+        for q in range(4):
             f = f + back_in[q, inv[q, k]]
         where = pl.ds(pl.multiple_of(k * BLOCK, BLOCK), BLOCK)
         out[:, where] = out[:, where] + f[0:3]
@@ -429,7 +449,7 @@
 
 def body(segments, pair_list, pair_count, send_list, cell_ids):
     segs = segments.shape[1]
-    a, b, p, own_sums, sure, far, mom, idx, inv = pl.pallas_call(
+    a, b, p, own_sums, sure, far, mom, idx, cnt, inv = pl.pallas_call(
         exchange,
         name="exchange",
         out_shape=(
@@ -440,11 +460,12 @@
             SDS((SURE, 2, 16, BLOCK), f32),
             SDS((OWN, 4, BLOCK), f32),
             SDS((NX, BLOCK), f32),
-            SDS((6, PAIRS), i32),
+            SDS((8, PAIRS), i32),
+            SDS((2, BLOCK), i32),
             SDS((4, BLOCK), i32),
         ),
         in_specs=[HB, HB, HB, HB, SM],
-        out_specs=(VM,) * 9,
+        out_specs=(VM,) * 10,
         scratch_shapes=[
             pltpu.VMEM((9, segs), f32),
             pltpu.VMEM((1, segs), i32),
@@ -465,28 +486,31 @@
             pltpu.VMEM((1, BLOCK), f32),
             pltpu.VMEM((NX, BLOCK), f32),
             pltpu.VMEM((GROUP, BLOCK, 2 * BLOCK), f32),
-            pltpu.VMEM((GROUP, 2 * BLOCK, BLOCK), bf16),
+            pltpu.VMEM((GROUP // 2, 2 * BLOCK, 2 * BLOCK), bf16),
             DMA((5,)), DMA((4,)), DMA((4,)), DMA((4,)), DMA((4,)), DMA, DMA, DMA, DMA,
         ],
         compiler_params=pltpu.CompilerParams(
             collective_id=0, has_side_effects=True, vmem_limit_bytes=24 * 2**20
         ),
-    )(segments, cell_ids.reshape(1, -1), send_list, pair_list.T, pair_count)
+    )(*[pltpu.with_memory_space_constraint(x, pltpu.HBM) for x in (segments, cell_ids.reshape(1, -1), send_list, pair_list.T)], pair_count)
     force = pl.pallas_call(
         pairs,
         name="pairs",
         out_shape=SDS((2 * ALL, 4, BLOCK), f32),
-        in_specs=[SM] + [VM] * 5,
+        in_specs=[SM] + [VM] * 6,
         out_specs=VM,
         scratch_shapes=[
+            pltpu.VMEM((8, PAIRS), i32),
+            pltpu.SMEM((8, PAIRS), i32),
             pltpu.VMEM((GROUP, BLOCK, 2 * BLOCK), f32),
-            pltpu.VMEM((GROUP, 2 * BLOCK, BLOCK), bf16),
+            pltpu.VMEM((GROUP // 2, 2 * BLOCK, 2 * BLOCK), bf16),
             pltpu.VMEM((GROUP, 2, 16, BLOCK), f32),
             pltpu.VMEM((2 * ALL + 1, 16, BLOCK), f32),
             pltpu.VMEM((2 * ALL + 1, 16, BLOCK), f32),
+            DMA,
         ],
         compiler_params=pltpu.CompilerParams(vmem_limit_bytes=24 * 2**20),
-    )(idx, a, b, p, own_sums, sure)
+    )(cnt, idx, a, b, p, own_sums, sure)
     return pl.pallas_call(
         finale,
         name="finale",

time: 58.9 us -> 44.9 us (0.76)
  Pallas kernels: 54.1 us -> 43.4 us
  local copies, waits for them, and re-layouts: 3.82 us -> 0.66 us
    pallas_call x1, Pallas kernels: 20.2 us -> 10.4 us  [body(): pl.pallas_call(finale, name='finale', out_shape=SDS((3, segs), f32), in_s...]
    pallas_call x1, Pallas kernels: 28 us -> 23.4 us  [body(): pl.pallas_call(exchange, name='exchange', out_shape=(SDS((SIB + OWN, BLOC...]
    pallas_call x1, Pallas kernels: 5.97 us -> 9.63 us  [body(): pl.pallas_call(pairs, name='pairs', out_shape=SDS((2 * ALL, 4, BLOCK), f3...]
    unnamed x9 -> x1, local copies, waits for them, and re-layouts: 3.82 us -> 0.66 us
where the time goes in v4:
time: 44.9 us; the launch traced here: 44.8 us
  Pallas kernels  43.4 us (97%)
  between operations  0.68 us (2%)
  local copies, waits for them, and re-layouts  0.66 us (1%)
    pallas_call x1, Pallas kernels, body(): pl.pallas_call(exchange, name='exchange', out_shape=(SDS((SIB + OWN, BLOC...  23.4 us
    pallas_call x1, Pallas kernels, body(): pl.pallas_call(finale, name='finale', out_shape=SDS((3, segs), f32), in_s...  10.4 us
    pallas_call x1, Pallas kernels, body(): pl.pallas_call(pairs, name='pairs', out_shape=SDS((2 * ALL, 4, BLOCK), f3...  9.63 us

profile of v4, /device:TPU:1, one launch (start us, length us, event | category | flops | bytes accessed | tf_op | source)
XLA Modules:
  0.0 44.8 jit_solution(18265790973222565539)
XLA Ops:
  0.7 23.4 %exchange.1 = (bf16[192,128,128]{2,1,0:T(8,128)(2,1)S(1)}, bf16[256,48,256]{2,1,0:T(8,128)(2,1)S(1)}, bf16[256,16,128]{2,1,0:T(8,128)(2,1)S(1)}, f32[64,16,128]{...) custom-call(f32[9,8192]{1,0:T(8,128)} %seg_in.1, ...), custom_call_target="tpu_custom_call" | custom-call | tf_op jit(solution)/shard_map/exchange/pallas_call | solution.py:452
  24.0 9.6 %pairs.1.force = f32[256,4,128]{2,1,0:T(4,128)S(1)} custom-call(s32[2,128]{1,0:T(2,128)S(1)} %get-tuple-element.18.counts, s32[8,512]{1,0:T(8,128)S(1)} %get-tuple-element.19.lists, bf16[192,128,128]{2,1,0:T(8,128)(2,1)S(1)} %get-tuple-element.20.a_ref, bf16[256,48,256]{2,1,0:T(8,128)(2,1)S(1)} %get-tuple-element.21.b_ref, ...), custom_call_target="tpu_custom_call" | custom-call | tf_op jit(solution)/shard_map/pairs/pallas_call | solution.py:496
  33.7 10.4 %finale.1 = f32[3,8192]{1,0:T(4,128)S(1)} custom-call(s32[4,128]{1,0:T(4,128)S(1)} %get-tuple-element.15.inv, f32[64,4,128]{2,1,0:T(4,128)S(1)} %get-tuple-element.16.far_ref, f32[8,128]{1,0:T(8,128)S(1)} %get-tuple-element.17.mom, f32[256,4,128]{2,1,0:T(4,128)S(1)} %pairs.1.force), custom_call_target="tpu_custom_call" | custom-call | tf_op jit(solution)/shard_map/finale/pallas_call | solution.py:514
  44.1 0.7 %copy.8 = f32[3,8192]{1,0:T(4,128)} copy(f32[3,8192]{1,0:T(4,128)S(1)} %finale.1) | data formatting | bytes 196608

commit v5 on v4

--- a/solution.py
+++ b/solution.py
@@ -113,6 +113,52 @@
         jnp.concatenate([w[r : r + BLOCK, 0:BLOCK].T, w[r : r + BLOCK, BLOCK:].T], axis=1) for r in (0, BLOCK)
     ]
     return sums_over(jnp.concatenate(turned, axis=0), p0, p1)
+
+
+def pipeline(groups, products, sums, close=None):
+    qd, ww = products.qd, products.ww
+
+    def step(c, b, a):
+        for s in range(0, GROUP, 2):
+            if c is not None:
+                sums(c * GROUP + s, s)
+            if b:
+                weigh(qd, ww, s)
+                weigh(qd, ww, s + 1)
+            if a is not None:
+                for d in range(2):
+                    products(a * GROUP + s + d, s + d)
+        if c is not None and close is not None:
+            close(c)
+
+    def body(t, _):
+        step(t - 2, True, t)
+        return 0
+
+    step(None, False, 0)
+    step(None, True, 1)
+    lax.fori_loop(2, groups, body, 0)
+    step(groups - 2, True, None)
+    step(groups - 1, False, None)
+
+
+class Products:
+    def __init__(self, qd, ww, a_ref, b_ref, pick):
+        self.qd, self.ww, self.a_ref, self.b_ref, self.pick = qd, ww, a_ref, b_ref, pick
+
+    def __call__(self, r, s):
+        i, j = self.pick(r)
+        self.qd[s] = mm(self.a_ref[i][:, 0:KDIM], spread(self.b_ref[j]))
+
+
+def along(ix, iy, o):
+    z, hi, core = iy // 4, lax.rem(iy // 2, 2), lax.rem(iy, 2)
+    return ix, lax.rem(z + o % 8, 8) * 4 + hi * 2 + lax.rem(core + o // 8, 2)
+
+
+def across(ix, iy, o):
+    z, hi, core = iy // 4, lax.rem(iy // 2, 2), lax.rem(iy, 2)
+    return lax.rem(ix + o % 8, 8), z * 4 + lax.rem(hi + o // 8, 2) * 2 + core
 
 
 def exchange(seg_in, cells_in, send_in, list_in, count, a_ref, b_ref, p_ref, self_ref, sure_ref, far_ref, mom_out,
@@ -131,16 +177,9 @@
         cp.start()
     barrier = pltpu.get_barrier_semaphore()
 
-    def greet_y(o, _):
-        pl.semaphore_signal(barrier, inc=1, device_id=(ix, lax.rem(iy + o, NY)), device_id_type=MESH)
-        return 0
-
-    def greet_x(o, _):
-        pl.semaphore_signal(barrier, inc=1, device_id=(lax.rem(ix + o, NX), iy), device_id_type=MESH)
-        return 0
-
-    lax.fori_loop(1, NY, greet_y, 0)
-    lax.fori_loop(1, NX, greet_x, 0)
+    other_y = (ix, lax.rem(iy + 2 * lax.rem(iy, 2) + NY - 1, NY))
+    for dev in [along(ix, iy, o) for o in range(1, 16)] + [across(ix, iy, o) for o in range(1, 16)] + [other_y]:
+        pl.semaphore_signal(barrier, inc=1, device_id=dev, device_id_type=MESH)
     cnt[...] = jnp.full((1, BLOCK), count[0], i32)
     for cp in loads:
         cp.wait()
@@ -162,7 +201,7 @@
     m1 = jnp.sum(jnp.where(cells[...] == first + 1, c, 0.0))
     mine = jnp.where(lanes == 2 * iy, m0, jnp.where(lanes == 2 * iy + 1, m1, 0.0))
     row[...] = mine
-    part[NY - 1 : NY, :] = mine
+    part[15:16, :] = mine
     centre, sib_centre = centre_of(ix, iy), centre_of(ix, sib[1])
     eye = eye128()
 
@@ -174,7 +213,7 @@
         return 0
 
     lax.fori_loop(0, OWN, build_own, 0, unroll=4)
-    pl.semaphore_wait(barrier, NY - 1 + NX - 1)
+    pl.semaphore_wait(barrier, 31)
     copies = []
     for q, dev in enumerate(neighbours(ix, iy)):
         copies.append(
@@ -185,14 +224,11 @@
         )
         copies[-1].start()
 
-    def send_y(o, _):
+    for o in range(1, 16):
         pltpu.make_async_remote_copy(
-            src_ref=row, dst_ref=part.at[pl.ds(o - 1, 1)], send_sem=s1, recv_sem=r1,
-            device_id=(ix, lax.rem(iy + o, NY)), device_id_type=MESH,
+            src_ref=row, dst_ref=part.at[o - 1 : o], send_sem=s1, recv_sem=r1,
+            device_id=along(ix, iy, o), device_id_type=MESH,
         ).start()
-        return 0
-
-    lax.fori_loop(1, NY, send_y, 0)
     shares = [
         pltpu.make_async_remote_copy(
             src_ref=src, dst_ref=dst, send_sem=ss.at[n], recv_sem=sr.at[n], device_id=sib, device_id_type=MESH
@@ -202,18 +238,10 @@
     for cp in shares[:3]:
         cp.start()
 
-    def step(t, _):
-        for s in range(0, GROUP, 2):
-            k = jnp.minimum(jnp.maximum((t - 2) * GROUP + s, 0), OWN - 2)
-            self_ref[k], self_ref[k + 1] = second_sums(ww, s // 2, p_ref[k], p_ref[k + 1])
-            weigh(qd, ww, s)
-            weigh(qd, ww, s + 1)
-            k = jnp.minimum(t * GROUP + s, OWN - 2)
-            qd[s] = mm(a_ref[k][:, 0:KDIM], spread(b_ref[k]))
-            qd[s + 1] = mm(a_ref[k + 1][:, 0:KDIM], spread(b_ref[k + 1]))
-        return 0
-
-    lax.fori_loop(0, OWN // GROUP + 2, step, 0)
+    def own_sums(k, s):
+        self_ref[k], self_ref[k + 1] = second_sums(ww, s // 2, p_ref[k], p_ref[k + 1])
+
+    pipeline(OWN // GROUP, Products(qd, ww, a_ref, b_ref, lambda k: (k, k)), own_sums)
     for cp in shares[:3]:
         cp.wait()
 
@@ -226,19 +254,15 @@
     for cp in copies:
         cp.wait()
     shares[3].start()
-    pltpu.make_async_copy(part.at[0 : NY - 1], part.at[0 : NY - 1], r1).wait()
+    pltpu.make_async_copy(part.at[0:15], part.at[0:15], r1).wait()
     slab = jnp.sum(part[...], axis=0, keepdims=True)
     row2[...] = slab
-    table[pl.ds(NX - 1, 1), :] = slab
-
-    def send_x(o, _):
+    table[15:16, :] = slab
+    for o in range(1, 16):
         pltpu.make_async_remote_copy(
-            src_ref=row2, dst_ref=table.at[pl.ds(o - 1, 1)], send_sem=s2, recv_sem=r2,
-            device_id=(lax.rem(ix + o, NX), iy), device_id_type=MESH,
+            src_ref=row2, dst_ref=table.at[o - 1 : o], send_sem=s2, recv_sem=r2,
+            device_id=across(ix, iy, o), device_id_type=MESH,
         ).start()
-        return 0
-
-    lax.fori_loop(1, NX, send_x, 0)
 
     def ghosts_of(buf, cen, base):
         def build(j, _):
@@ -253,19 +277,11 @@
 
     ghosts_of(in_buf, centre, OWN)
 
-    def sure_step(t, _):
-        for s in range(0, GROUP, 2):
-            k = jnp.minimum(jnp.maximum((t - 2) * GROUP + s, 0), SURE - 2)
-            sure_ref[k, 0], sure_ref[k + 1, 0] = first_sums(ww, s // 2, p_ref[plist[1, k]], p_ref[plist[1, k + 1]])
-            sure_ref[k, 1], sure_ref[k + 1, 1] = second_sums(ww, s // 2, p_ref[plist[0, k]], p_ref[plist[0, k + 1]])
-            weigh(qd, ww, s)
-            weigh(qd, ww, s + 1)
-            k = jnp.minimum(t * GROUP + s, SURE - 2)
-            for d in range(2):
-                qd[s + d] = mm(a_ref[plist[0, k + d]][:, 0:KDIM], spread(b_ref[plist[1, k + d]]))
-        return 0
-
-    lax.fori_loop(0, SURE // GROUP + 2, sure_step, 0)
+    def sure_sums(k, s):
+        sure_ref[k, 0], sure_ref[k + 1, 0] = first_sums(ww, s // 2, p_ref[plist[1, k]], p_ref[plist[1, k + 1]])
+        sure_ref[k, 1], sure_ref[k + 1, 1] = second_sums(ww, s // 2, p_ref[plist[0, k]], p_ref[plist[0, k + 1]])
+
+    pipeline(SURE // GROUP, Products(qd, ww, a_ref, b_ref, lambda k: (plist[0, k], plist[1, k])), sure_sums)
     idx_out[0:2, :] = ids[...]
     idx_out[2:4, :] = sib_ids[...] + SIB
     idx_out[4:8, :] = jnp.zeros((4, PAIRS), i32)
@@ -273,10 +289,10 @@
     cnt_out[1:2, :] = sib_cnt[...]
     shares[3].wait()
     ghosts_of(sib_ghost, sib_centre, SIB + OWN)
-    pltpu.make_async_copy(table.at[0 : NX - 1], table.at[0 : NX - 1], r2).wait()
-    mom_out[...] = table[...]
-    pltpu.make_async_copy(part.at[0 : NY - 1], part.at[0 : NY - 1], s1).wait()
-    pltpu.make_async_copy(table.at[0 : NX - 1], table.at[0 : NX - 1], s2).wait()
+    pltpu.make_async_copy(table.at[0:15], table.at[0:15], r2).wait()
+    mom_out[...] = table[0:NX, :] + table[NX:, :]
+    pltpu.make_async_copy(part.at[0:15], part.at[0:15], s1).wait()
+    pltpu.make_async_copy(table.at[0:15], table.at[0:15], s2).wait()
 
 
 def finish(acc, p):
@@ -291,11 +307,10 @@
     n_own = jnp.minimum(own_rows, half)
     n_help = jnp.maximum(sib_rows - half, 0)
     total = n_own + n_help
-    r = lax.broadcasted_iota(i32, (1, PAIRS), 1) - 2 * GROUP
-    skip = SURE - 2 * GROUP
-    own_list = pltpu.roll(lists[...], PAIRS - skip, 1)
-    sib_list = pltpu.roll(lists[...], PAIRS - (skip + half - n_own), 1)
-    live = jnp.logical_and(r >= 0, r < total)
+    r = lax.broadcasted_iota(i32, (1, PAIRS), 1)
+    own_list = pltpu.roll(lists[...], PAIRS - SURE, 1)
+    sib_list = pltpu.roll(lists[...], PAIRS - (SURE + half - n_own), 1)
+    live = r < total
     i = jnp.where(r < n_own, own_list[0:1], sib_list[2:3])
     j = jnp.where(r < n_own, own_list[1:2], sib_list[3:4])
     merged[0:1, :] = jnp.where(live, i, 0)
@@ -324,25 +339,17 @@
 
     lax.fori_loop(0, SURE, add_sure, 0, unroll=8)
 
-    def step(t, _):
-        for s in range(0, GROUP, 2):
-            c = t * GROUP + s
-            rr[s, 0], rr[s + 1, 0] = first_sums(ww, s // 2, p_ref[rows[1, c]], p_ref[rows[1, c + 1]])
-            rr[s, 1], rr[s + 1, 1] = second_sums(ww, s // 2, p_ref[rows[0, c]], p_ref[rows[0, c + 1]])
-            weigh(qd, ww, s)
-            weigh(qd, ww, s + 1)
-            c = c + 2 * GROUP
-            for d in range(2):
-                qd[s + d] = mm(a_ref[rows[0, c + d]][:, 0:KDIM], spread(b_ref[rows[1, c + d]]))
+    def sums(c, s):
+        rr[s, 0], rr[s + 1, 0] = first_sums(ww, s // 2, p_ref[rows[1, c]], p_ref[rows[1, c + 1]])
+        rr[s, 1], rr[s + 1, 1] = second_sums(ww, s // 2, p_ref[rows[0, c]], p_ref[rows[0, c + 1]])
+
+    def close(t):
         for s in range(GROUP):
-            c = t * GROUP + s
-            acc_a[rows[2, c]] += rr[s, 0]
-            acc_b[rows[3, c]] += rr[s, 1]
-        return 0
-
-    @pl.when(total > 0)
-    def _():
-        lax.fori_loop(0, (total + GROUP - 1) // GROUP + 2, step, 0)
+            acc_a[rows[2, t * GROUP + s]] += rr[s, 0]
+            acc_b[rows[3, t * GROUP + s]] += rr[s, 1]
+
+    products = Products(qd, ww, a_ref, b_ref, lambda c: (rows[0, c], rows[1, c]))
+    pipeline(jnp.maximum((total + GROUP - 1) // GROUP, 2), products, sums, close)
 
     def finish_own(k, _):
         out[k] = finish(acc_a[k] + acc_b[k], p_ref[k])
@@ -482,9 +489,9 @@
             pltpu.VMEM((4, ROWS, BLOCK), f32),
             pltpu.VMEM((4, ROWS, BLOCK), f32),
             pltpu.VMEM((1, BLOCK), f32),
-            pltpu.VMEM((NY, BLOCK), f32),
+            pltpu.VMEM((16, BLOCK), f32),
             pltpu.VMEM((1, BLOCK), f32),
-            pltpu.VMEM((NX, BLOCK), f32),
+            pltpu.VMEM((16, BLOCK), f32),
             pltpu.VMEM((GROUP, BLOCK, 2 * BLOCK), f32),
             pltpu.VMEM((GROUP // 2, 2 * BLOCK, 2 * BLOCK), bf16),
             DMA((5,)), DMA((4,)), DMA((4,)), DMA((4,)), DMA((4,)), DMA, DMA, DMA, DMA,

time: 44.9 us -> 45.6 us (1.016)
  the two profiles are of different devices: /device:TPU:1 before, /device:TPU:13 now
where the time goes in v5:
time: 45.6 us; the launch traced here: 45.5 us
  Pallas kernels  44.2 us (97%)
  between operations  0.68 us (1%)
  local copies, waits for them, and re-layouts  0.66 us (1%)
    pallas_call x1, Pallas kernels, body(): pl.pallas_call(finale, name='finale', out_shape=SDS((3, segs), f32), in_s...  21.3 us
    pallas_call x1, Pallas kernels, body(): pl.pallas_call(exchange, name='exchange', out_shape=(SDS((SIB + OWN, BLOC...  18.3 us
    pallas_call x1, Pallas kernels, body(): pl.pallas_call(pairs, name='pairs', out_shape=SDS((2 * ALL, 4, BLOCK), f3...  4.55 us

profile of v5, /device:TPU:13, one launch (start us, length us, event | category | flops | bytes accessed | tf_op | source)
XLA Modules:
  0.0 45.5 jit_solution(5972620229522833892)
XLA Ops:
  0.7 18.3 %exchange.1 = (bf16[192,128,128]{2,1,0:T(8,128)(2,1)S(1)}, bf16[256,48,256]{2,1,0:T(8,128)(2,1)S(1)}, bf16[256,16,128]{2,1,0:T(8,128)(2,1)S(1)}, f32[64,16,128]{...) custom-call(f32[9,8192]{1,0:T(8,128)} %seg_in.1, ...), custom_call_target="tpu_custom_call" | custom-call | tf_op jit(solution)/shard_map/exchange/pallas_call | solution.py:459
  18.9 4.6 %pairs.1.force = f32[256,4,128]{2,1,0:T(4,128)S(1)} custom-call(s32[2,128]{1,0:T(2,128)S(1)} %get-tuple-element.18.counts, s32[8,512]{1,0:T(8,128)S(1)} %get-tuple-element.19.lists, bf16[192,128,128]{2,1,0:T(8,128)(2,1)S(1)} %get-tuple-element.20.a_ref, bf16[256,48,256]{2,1,0:T(8,128)(2,1)S(1)} %get-tuple-element.21.b_ref, ...), custom_call_target="tpu_custom_call" | custom-call | tf_op jit(solution)/shard_map/pairs/pallas_call | solution.py:503
  23.5 21.3 %finale.1 = f32[3,8192]{1,0:T(4,128)S(1)} custom-call(s32[4,128]{1,0:T(4,128)S(1)} %get-tuple-element.15.inv, f32[64,4,128]{2,1,0:T(4,128)S(1)} %get-tuple-element.16.far_ref, f32[8,128]{1,0:T(8,128)S(1)} %get-tuple-element.17.mom, f32[256,4,128]{2,1,0:T(4,128)S(1)} %pairs.1.force), custom_call_target="tpu_custom_call" | custom-call | tf_op jit(solution)/shard_map/finale/pallas_call | solution.py:521
  44.9 0.7 %copy.8 = f32[3,8192]{1,0:T(4,128)} copy(f32[3,8192]{1,0:T(4,128)S(1)} %finale.1) | data formatting | bytes 196608

commit v6 on v5

--- a/solution.py
+++ b/solution.py
@@ -212,8 +212,13 @@
         far_ref[k] = jnp.concatenate([raw[0:2], raw[2:3] - 0.5, weight], axis=0)
         return 0
 
-    lax.fori_loop(0, OWN, build_own, 0, unroll=4)
+    lax.fori_loop(0, OWN, build_own, 0, unroll=8)
     pl.semaphore_wait(barrier, 31)
+    for o in range(1, 16):
+        pltpu.make_async_remote_copy(
+            src_ref=row, dst_ref=part.at[o - 1 : o], send_sem=s1, recv_sem=r1,
+            device_id=along(ix, iy, o), device_id_type=MESH,
+        ).start()
     copies = []
     for q, dev in enumerate(neighbours(ix, iy)):
         copies.append(
@@ -224,11 +229,6 @@
         )
         copies[-1].start()
 
-    for o in range(1, 16):
-        pltpu.make_async_remote_copy(
-            src_ref=row, dst_ref=part.at[o - 1 : o], send_sem=s1, recv_sem=r1,
-            device_id=along(ix, iy, o), device_id_type=MESH,
-        ).start()
     shares = [
         pltpu.make_async_remote_copy(
             src_ref=src, dst_ref=dst, send_sem=ss.at[n], recv_sem=sr.at[n], device_id=sib, device_id_type=MESH
@@ -250,10 +250,7 @@
         features(raw, sib_centre, eye, a_ref, b_ref, p_ref, SIB + k, True)
         return 0
 
-    lax.fori_loop(0, OWN, build_sib, 0, unroll=4)
-    for cp in copies:
-        cp.wait()
-    shares[3].start()
+    lax.fori_loop(0, OWN, build_sib, 0, unroll=8)
     pltpu.make_async_copy(part.at[0:15], part.at[0:15], r1).wait()
     slab = jnp.sum(part[...], axis=0, keepdims=True)
     row2[...] = slab
@@ -264,6 +261,9 @@
             device_id=across(ix, iy, o), device_id_type=MESH,
         ).start()
 
+    for cp in copies:
+        cp.wait()
+    shares[3].start()
     def ghosts_of(buf, cen, base):
         def build(j, _):
             for q in range(4):
@@ -273,7 +273,7 @@
                 features(raw, cen, eye, a_ref, b_ref, p_ref, base + GHOST * q + j, False)
             return 0
 
-        lax.fori_loop(0, GHOST, build, 0)
+        lax.fori_loop(0, GHOST, build, 0, unroll=2)
 
     ghosts_of(in_buf, centre, OWN)
 
@@ -359,8 +359,8 @@
         out[k] = finish(acc_b[k], p_ref[k])
         return 0
 
-    lax.fori_loop(0, OWN, finish_own, 0, unroll=4)
-    lax.fori_loop(OWN, ALL, finish_other, 0, unroll=4)
+    lax.fori_loop(0, OWN, finish_own, 0, unroll=8)
+    lax.fori_loop(OWN, ALL, finish_other, 0, unroll=8)
 
     @pl.when(n_help > 0)
     def _():
@@ -372,21 +372,49 @@
         out[SIB:] = jnp.zeros((ALL, 4, BLOCK), f32)
 
 
-def finale(inv, far_ref, mom, force, out, sib_in, gsum, back_in, mb, ss, sr, s_sem, r_sem):
+def finale(inv, far_ref, mom, force, out, sib_in, back_in, mb, ss, sr, s_sem, r_sem):
     ix, iy = lax.axis_index("gx"), lax.axis_index("gy")
-    sib = (ix, iy + 1 - 2 * lax.rem(iy, 2))
+    core = lax.rem(iy, 2)
+    sy = iy + 1 - 2 * core
+    lower, upper = lax.rem(ix + NX - 1, NX), lax.rem(ix + 1, NX)
+    step = 2 * core - 1
+    beyond = lax.rem(iy + step + NY, NY)
+    sib_beyond = lax.rem(sy - step + NY, NY)
+    beyond_sib = lax.rem(iy + 2 * step + NY, NY)
     barrier = pltpu.get_barrier_semaphore()
-    near = neighbours(ix, iy)
-    for dev in near:
+    peers = [(lower, iy), (upper, iy), (ix, sy), (ix, beyond), (lower, sy), (upper, sy), (ix, sib_beyond), (ix, beyond_sib)]
+    for dev in peers:
         pl.semaphore_signal(barrier, inc=1, device_id=dev, device_id_type=MESH)
-    for q in range(4):
-        back_in[q, GHOST] = jnp.zeros((4, BLOCK), f32)
-    pl.semaphore_wait(barrier, 4)
+    for n in range(8):
+        back_in[n, GHOST] = jnp.zeros((4, BLOCK), f32)
+    near_side, away_side = OWN + GHOST * (3 - core), OWN + GHOST * (2 + core)
+    sib_near, sib_away = SIB + OWN + GHOST * (2 + core), SIB + OWN + GHOST * (3 - core)
+    pl.semaphore_wait(barrier, 8)
     share = pltpu.make_async_remote_copy(
-        src_ref=force.at[SIB : SIB + ALL], dst_ref=sib_in, send_sem=ss, recv_sem=sr, device_id=sib,
+        src_ref=force.at[SIB : SIB + OWN], dst_ref=sib_in, send_sem=ss, recv_sem=sr, device_id=(ix, sy),
         device_id_type=MESH,
     )
+    sends = (
+        (OWN, 1, (lower, iy)),
+        (OWN + GHOST, 0, (upper, iy)),
+        (away_side, 3, (ix, beyond)),
+        (SIB + OWN, 5, (lower, sy)),
+        (SIB + OWN + GHOST, 4, (upper, sy)),
+        (sib_away, 7, (ix, sib_beyond)),
+        (near_side, 2, (ix, sy)),
+    )
+    copies = [
+        pltpu.make_async_remote_copy(
+            src_ref=force.at[pl.ds(start, GHOST)], dst_ref=back_in.at[slot, 0:GHOST], send_sem=s_sem.at[slot],
+            recv_sem=r_sem.at[slot], device_id=dev, device_id_type=MESH,
+        )
+        for start, slot, dev in sends
+    ]
+    for cp in copies:
+        cp.start()
     share.start()
+    for j in range(GHOST):
+        back_in[6, j] = force[sib_near + j]
     wide = jnp.concatenate([mom[...], jnp.zeros((BLOCK - NX, BLOCK), f32)], axis=0).T
     for s in range(NX):
         mb[s] = jnp.broadcast_to(wide[0 : 2 * NY, s : s + 1], (2 * NY, BLOCK))
@@ -420,32 +448,21 @@
         out[:, where] = blk[3:4] * f
         return 0
 
-    lax.fori_loop(0, OWN // 4, far, 0)
-    share.wait()
-    gsum[...] = force[OWN:ALL] + sib_in[OWN:ALL]
-    copies = []
-    for q, dev in enumerate(near):
-        copies.append(
-            pltpu.make_async_remote_copy(
-                src_ref=gsum.at[GHOST * q : GHOST * q + GHOST], dst_ref=back_in.at[q ^ 1, 0:GHOST],
-                send_sem=s_sem.at[q], recv_sem=r_sem.at[q ^ 1], device_id=dev, device_id_type=MESH,
-            )
-        )
-        copies[-1].start()
-
-    lax.fori_loop(OWN // 4, OWN, far, 0)
+    lax.fori_loop(0, OWN, far, 0)
     for cp in copies:
         cp.wait()
+    share.wait()
+    lists = (0, 1, 3 - core, 2 + core, 0, 1, 3 - core, 2 + core)
 
     def combine(k, _):
         f = force[k] + sib_in[k]
-        for q in range(4):
-            f = f + back_in[q, inv[q, k]]
+        for n, q in enumerate(lists):
+            f = f + back_in[n, inv[q, k]]
         where = pl.ds(pl.multiple_of(k * BLOCK, BLOCK), BLOCK)
         out[:, where] = out[:, where] + f[0:3]
         return 0
 
-    lax.fori_loop(0, OWN, combine, 0, unroll=4)
+    lax.fori_loop(0, OWN, combine, 0, unroll=8)
 
 
 VM, SM = pl.BlockSpec(memory_space=pltpu.VMEM), pl.BlockSpec(memory_space=pltpu.SMEM)
@@ -525,11 +542,10 @@
         in_specs=[SM, VM, VM, VM],
         out_specs=VM,
         scratch_shapes=[
-            pltpu.VMEM((ALL, 4, BLOCK), f32),
-            pltpu.VMEM((4 * GHOST, 4, BLOCK), f32),
-            pltpu.VMEM((4, GHOST + 1, 4, BLOCK), f32),
+            pltpu.VMEM((OWN, 4, BLOCK), f32),
+            pltpu.VMEM((8, GHOST + 1, 4, BLOCK), f32),
             pltpu.VMEM((NX, 2 * NY, BLOCK), f32),
-            DMA, DMA, DMA((4,)), DMA((4,)),
+            DMA, DMA, DMA((8,)), DMA((8,)),
         ],
         compiler_params=pltpu.CompilerParams(
             collective_id=1, has_side_effects=True, vmem_limit_bytes=16 * 2**20

time: 45.6 us -> 40.8 us (0.89)
  the two profiles are of different devices: /device:TPU:13 before, /device:TPU:1 now
where the time goes in v6:
time: 40.8 us; the launch traced here: 40.4 us
  Pallas kernels  39.1 us (96%)
  between operations  0.68 us (2%)
  local copies, waits for them, and re-layouts  0.66 us (2%)
    pallas_call x1, Pallas kernels, body(): pl.pallas_call(exchange, name='exchange', out_shape=(SDS((SIB + OWN, BLOC...  20.2 us
    pallas_call x1, Pallas kernels, body(): pl.pallas_call(finale, name='finale', out_shape=SDS((3, segs), f32), in_s...  10.1 us
    pallas_call x1, Pallas kernels, body(): pl.pallas_call(pairs, name='pairs', out_shape=SDS((2 * ALL, 4, BLOCK), f3...  8.8 us

profile of v6, /device:TPU:1, one launch (start us, length us, event | category | flops | bytes accessed | tf_op | source)
XLA Modules:
  0.0 40.4 jit_solution(5811968923039446810)
XLA Ops:
  0.7 20.2 %exchange.1 = (bf16[192,128,128]{2,1,0:T(8,128)(2,1)S(1)}, bf16[256,48,256]{2,1,0:T(8,128)(2,1)S(1)}, bf16[256,16,128]{2,1,0:T(8,128)(2,1)S(1)}, f32[64,16,128]{...) custom-call(f32[9,8192]{1,0:T(8,128)} %seg_in.1, ...), custom_call_target="tpu_custom_call" | custom-call | tf_op jit(solution)/shard_map/exchange/pallas_call | solution.py:476
  20.8 8.8 %pairs.1.force = f32[256,4,128]{2,1,0:T(4,128)S(1)} custom-call(s32[2,128]{1,0:T(2,128)S(1)} %get-tuple-element.18.counts, s32[8,512]{1,0:T(8,128)S(1)} %get-tuple-element.19.lists, bf16[192,128,128]{2,1,0:T(8,128)(2,1)S(1)} %get-tuple-element.20.a_ref, bf16[256,48,256]{2,1,0:T(8,128)(2,1)S(1)} %get-tuple-element.21.b_ref, ...), custom_call_target="tpu_custom_call" | custom-call | tf_op jit(solution)/shard_map/pairs/pallas_call | solution.py:520
  29.6 10.1 %finale.1 = f32[3,8192]{1,0:T(4,128)S(1)} custom-call(s32[4,128]{1,0:T(4,128)S(1)} %get-tuple-element.15.inv, f32[64,4,128]{2,1,0:T(4,128)S(1)} %get-tuple-element.16.far_ref, f32[8,128]{1,0:T(8,128)S(1)} %get-tuple-element.17.mom, f32[256,4,128]{2,1,0:T(4,128)S(1)} %pairs.1.force), custom_call_target="tpu_custom_call" | custom-call | tf_op jit(solution)/shard_map/finale/pallas_call | solution.py:538
  39.7 0.7 %copy.8 = f32[3,8192]{1,0:T(4,128)} copy(f32[3,8192]{1,0:T(4,128)S(1)} %finale.1) | data formatting | bytes 196608

commit v7 on v6

--- a/solution.py
+++ b/solution.py
@@ -212,7 +212,7 @@
         far_ref[k] = jnp.concatenate([raw[0:2], raw[2:3] - 0.5, weight], axis=0)
         return 0
 
-    lax.fori_loop(0, OWN, build_own, 0, unroll=8)
+    lax.fori_loop(0, OWN, build_own, 0, unroll=16)
     pl.semaphore_wait(barrier, 31)
     for o in range(1, 16):
         pltpu.make_async_remote_copy(
@@ -250,7 +250,7 @@
         features(raw, sib_centre, eye, a_ref, b_ref, p_ref, SIB + k, True)
         return 0
 
-    lax.fori_loop(0, OWN, build_sib, 0, unroll=8)
+    lax.fori_loop(0, OWN, build_sib, 0, unroll=16)
     pltpu.make_async_copy(part.at[0:15], part.at[0:15], r1).wait()
     slab = jnp.sum(part[...], axis=0, keepdims=True)
     row2[...] = slab
@@ -273,7 +273,7 @@
                 features(raw, cen, eye, a_ref, b_ref, p_ref, base + GHOST * q + j, False)
             return 0
 
-        lax.fori_loop(0, GHOST, build, 0, unroll=2)
+        lax.fori_loop(0, GHOST, build, 0, unroll=4)
 
     ghosts_of(in_buf, centre, OWN)
 
@@ -448,7 +448,7 @@
         out[:, where] = blk[3:4] * f
         return 0
 
-    lax.fori_loop(0, OWN, far, 0)
+    lax.fori_loop(0, OWN, far, 0, unroll=2)
     for cp in copies:
         cp.wait()
     share.wait()

time: 40.8 us -> 40.1 us (0.983)
  the two profiles are of different devices: /device:TPU:1 before, /device:TPU:59 now
where the time goes in v7:
time: 40.1 us; the launch traced here: 40 us
  Pallas kernels  38.7 us (97%)
  between operations  0.68 us (2%)
  local copies, waits for them, and re-layouts  0.66 us (2%)
    pallas_call x1, Pallas kernels, body(): pl.pallas_call(finale, name='finale', out_shape=SDS((3, segs), f32), in_s...  15.7 us
    pallas_call x1, Pallas kernels, body(): pl.pallas_call(exchange, name='exchange', out_shape=(SDS((SIB + OWN, BLOC...  15.6 us
    pallas_call x1, Pallas kernels, body(): pl.pallas_call(pairs, name='pairs', out_shape=SDS((2 * ALL, 4, BLOCK), f3...  7.42 us

profile of v7, /device:TPU:59, one launch (start us, length us, event | category | flops | bytes accessed | tf_op | source)
XLA Modules:
  0.0 40.0 jit_solution(7818750191184210672)
XLA Ops:
  0.7 15.6 %exchange.1 = (bf16[192,128,128]{2,1,0:T(8,128)(2,1)S(1)}, bf16[256,48,256]{2,1,0:T(8,128)(2,1)S(1)}, bf16[256,16,128]{2,1,0:T(8,128)(2,1)S(1)}, f32[64,16,128]{...) custom-call(f32[9,8192]{1,0:T(8,128)} %seg_in.1, ...), custom_call_target="tpu_custom_call" | custom-call | tf_op jit(solution)/shard_map/exchange/pallas_call | solution.py:476
  16.2 7.4 %pairs.1.force = f32[256,4,128]{2,1,0:T(4,128)S(1)} custom-call(s32[2,128]{1,0:T(2,128)S(1)} %get-tuple-element.18.counts, s32[8,512]{1,0:T(8,128)S(1)} %get-tuple-element.19.lists, bf16[192,128,128]{2,1,0:T(8,128)(2,1)S(1)} %get-tuple-element.20.a_ref, bf16[256,48,256]{2,1,0:T(8,128)(2,1)S(1)} %get-tuple-element.21.b_ref, ...), custom_call_target="tpu_custom_call" | custom-call | tf_op jit(solution)/shard_map/pairs/pallas_call | solution.py:520
  23.6 15.7 %finale.1 = f32[3,8192]{1,0:T(4,128)S(1)} custom-call(s32[4,128]{1,0:T(4,128)S(1)} %get-tuple-element.15.inv, f32[64,4,128]{2,1,0:T(4,128)S(1)} %get-tuple-element.16.far_ref, f32[8,128]{1,0:T(8,128)S(1)} %get-tuple-element.17.mom, f32[256,4,128]{2,1,0:T(4,128)S(1)} %pairs.1.force), custom_call_target="tpu_custom_call" | custom-call | tf_op jit(solution)/shard_map/finale/pallas_call | solution.py:538
  39.4 0.7 %copy.8 = f32[3,8192]{1,0:T(4,128)} copy(f32[3,8192]{1,0:T(4,128)S(1)} %finale.1) | data formatting | bytes 196608
